TPU v7x, 256 devices: a whole 4x4x8 slice. The times are simulated.
256 devices in a mesh: camtime: 16 (over z, x_lo), heads: 16 (over x_hi, y, core).
Axes of the slice: x: 4 (x_hi: 2, x_lo: 2; x = x_hi * 2 + x_lo), y: 4, z: 8, core: 2. Of those that a mesh axis runs over, the one named last changes fastest.
Arguments:
- hidden_patch_vectors: bfloat16 [16, 6, 128, 2048], P('camtime', None, None, 'heads'), may hold values from -6 to 6
- entry_rms_multiplier: float32 [2048], replicated, may hold values from 0.1 to 1.9
- lookup_projection_matrix: bfloat16 [2048, 3, 2048], P(None, None, 'heads')
- exit_projection_matrix: bfloat16 [2048, 2048], P('heads'), may hold values from -0.5 to 0.5
- probe_sharpness: float32 [16], P('heads'), may hold values from 0.5 to 32
- adjacent_camera_pairs: int32 [6, 2], replicated, may hold values from 0 to 5, as said below
- prior_frame_allowed: int32 [16, 6], replicated, may hold values 0 or 1
Outputs:
- attended: bfloat16 [16, 6, 128, 2048], P('camtime', None, None, 'heads')
Inputs may be any that keep to these rules, and one draw needn't show every extreme that they name: adjacent_camera_pairs[c, 0] and adjacent_camera_pairs[c, 1] are the cameras before and after camera c on one loop that passes through all 6 cameras once.
All inputs are finite; a program needn't handle non-finite values.
Results may differ from a plain program's by a relative error of at most 0.018.
The roundings to bfloat16 on the way count: a program that leaves them out, or rounds other values in their place, can miss the bound.
Values may be sent and summed in bfloat16 or wider, within the bound.
A program may use at most 64 MiB of HBM per device.

v0:
```python
import jax
import jax.numpy as jnp
from jax import lax
from jax.sharding import PartitionSpec as P

PROBE_DEPTH = 128


def unit_rows(raw):
    return (raw * lax.rsqrt(jnp.mean(raw * raw, axis=-1, keepdims=True) + 1e-06)).astype(
        jnp.bfloat16
    )


def on_device(
    hidden_patch_vectors,
    entry_rms_multiplier,
    lookup_projection_matrix,
    exit_projection_matrix,
    probe_sharpness,
    adjacent_camera_pairs,
    prior_frame_allowed,
):
    frames_dev, cams, patches, local_width = hidden_patch_vectors.shape
    width = entry_rms_multiplier.shape[0]
    local_heads = local_width // PROBE_DEPTH
    total_rows = frames_dev * cams * patches
    tokens = hidden_patch_vectors.reshape(total_rows, local_width)
    w_flat = lookup_projection_matrix.reshape(width, 3 * local_width)
    wide = lax.all_gather(tokens, "heads", axis=1, tiled=True).astype(jnp.float32)
    scaled = (wide * entry_rms_multiplier[None, :]).astype(jnp.bfloat16)
    accum = jnp.dot(scaled, w_flat, preferred_element_type=jnp.float32)
    accum, squares = (accum, jnp.sum(wide * wide, axis=1))
    inv_rms = lax.rsqrt(squares / width + 1e-06)
    raw = (accum * inv_rms[:, None]).reshape(frames_dev, cams, patches, 3, local_heads, PROBE_DEPTH)
    query = unit_rows(raw[:, :, :, 0])
    key = unit_rows(raw[:, :, :, 1])
    value = raw[:, :, :, 2].astype(jnp.bfloat16)
    cam_ids = jnp.arange(cams, dtype=jnp.int32)
    index_table = jnp.concatenate([cam_ids[:, None], adjacent_camera_pairs], axis=1)
    select = (index_table[:, :, None] == cam_ids[None, None, :]).astype(jnp.bfloat16)
    k_cross = jnp.einsum(
        "cjn,fnphe->fcjphe", select, key, preferred_element_type=jnp.float32
    ).astype(jnp.bfloat16)
    v_cross = jnp.einsum(
        "cjn,fnphe->fcjphe", select, value, preferred_element_type=jnp.float32
    ).astype(jnp.bfloat16)
    k_cross = k_cross.reshape(frames_dev, cams, 3 * patches, local_heads, PROBE_DEPTH)
    v_cross = v_cross.reshape(frames_dev, cams, 3 * patches, local_heads, PROBE_DEPTH)
    exponent_divisor = (probe_sharpness / jnp.sqrt(jnp.float32(PROBE_DEPTH)))[
        None, None, :, None, None
    ]
    score = (
        jnp.einsum("fcphe,fckhe->fchpk", query, k_cross, preferred_element_type=jnp.float32)
        * exponent_divisor
    )
    top = jnp.max(score, axis=4)
    expo = jnp.exp(score - top[..., None])
    total = jnp.sum(expo, axis=4)
    summed = jnp.einsum(
        "fchpk,fckhe->fchpe", expo.astype(jnp.bfloat16), v_cross, preferred_element_type=jnp.float32
    )
    position = lax.axis_index("camtime")
    own_frames = position * frames_dev + jnp.arange(frames_dev, dtype=jnp.int32)
    kv_pairs = jnp.stack([key, value], axis=1)
    kv_piece = lax.all_gather(kv_pairs, "camtime", axis=0, tiled=True)

    def one(step, state):
        top_now, total_now, summed_now = state
        pair = lax.dynamic_index_in_dim(kv_piece, step, 0, keepdims=False)
        mask_row = lax.dynamic_index_in_dim(
            prior_frame_allowed,
            jnp.clip(step, 0, prior_frame_allowed.shape[0] - 1),
            0,
            keepdims=False,
        )
        valid = (step >= 0) & (step < own_frames)[:, None] & (mask_row == 1)[None, :]
        s_time = (
            jnp.einsum("fcphe,cqhe->fchpq", query, pair[0], preferred_element_type=jnp.float32)
            * exponent_divisor
        )
        s_time = jnp.where(valid[:, :, None, None, None], s_time, -jnp.inf)
        top_next = jnp.maximum(top_now, jnp.max(s_time, axis=4))
        rescale = jnp.exp(top_now - top_next)
        expo_time = jnp.exp(s_time - top_next[..., None])
        total_next = total_now * rescale + jnp.sum(expo_time, axis=4)
        summed_next = summed_now * rescale[..., None] + jnp.einsum(
            "fchpq,cqhe->fchpe",
            expo_time.astype(jnp.bfloat16),
            pair[1],
            preferred_element_type=jnp.float32,
        )
        return (top_next, total_next, summed_next)

    top, total, summed = lax.fori_loop(0, kv_piece.shape[0], one, (top, total, summed))
    mixed = (summed / total[..., None]).astype(jnp.bfloat16)
    mixed = jnp.transpose(mixed, (0, 1, 3, 2, 4)).reshape(total_rows, local_width)
    partial_value = jnp.dot(mixed, exit_projection_matrix, preferred_element_type=jnp.float32)
    result = lax.psum_scatter(
        partial_value.astype(jnp.bfloat16), "heads", scatter_dimension=1, tiled=True
    )
    return result.reshape(frames_dev, cams, patches, local_width)


def solution(mesh):
    placed = (
        P("camtime", None, None, "heads"),
        P(),
        P(None, None, "heads"),
        P("heads", None),
        P("heads"),
        P(),
        P(),
    )
    return jax.shard_map(
        on_device,
        mesh=mesh,
        in_specs=placed,
        out_specs=P("camtime", None, None, "heads"),
        check_vma=False,
    )
```

profile of v0, /device:TPU:193, one launch (start us, length us, event | category | flops | bytes accessed | tf_op | source)
XLA Modules:
  0.0 358.2 jit_solution(15536292400397349384)
XLA Ops:
  7.3 1.7 copy.53
  9.1 59.0 %all-gather.3.cloned.1.call-done = bf16[768,2048]{1,0:T(8,128)(2,1)} async-done(((bf16[768,128]{1,0:T(8,128)(2,1)}), bf16[768,2048]{1,0:T(8,128)(2,1)}) %all-gather.3.cloned.1.call-update) | async-done | bytes 3145744 | tf_op jit(solution)/shard_map/all_gather | solution.py:30
  68.0 2.7 fusion.14
  70.9 2.9 fusion.18
  73.7 1.6 copy.54
  84.8 133.3 %all-gather.5.cloned.1.call-done = bf16[16,2,6,128,1,128]{5,3,4,2,1,0:T(8,128)(2,1)} async-done(((bf16[1,2,6,128,1,128]{5,3,4,2,1,0:T(8,128)(2,1)}), bf16[16,2,6,128,1,128]{5,3,4,2,1,0:T(8,128)(2,1)}) %all-gather.5.cloned.1.call-update) | async-done | bytes 6291472 | tf_op jit(solution)/shard_map/all_gather | solution.py:66
  218.1 42.0 %while.17 = (s32[]{:T(128)}, f32[1,6,1,128]{3,1,2,0:T(8,128)S(1)}, f32[1,6,1,128]{3,1,2,0:T(8,128)S(1)}, f32[1,6,1,128,128]{3,4,1,0,2:T(8,128)S(1)}, s32[1]{0:T(...) while((s32[]{:T(128)}, f32[1,6,1,128]{3,1,2,0:T(8,128)S(1)}, ...), condition=%wide.region_8.9_spmd, body=%wide.region_5.8_spmd.sunk | while | flops 51218708 | bytes 2606819 | solution.py:95
  219.4 1.3 fusion.59
  222.0 1.3 fusion.59
  224.6 1.3 fusion.59
  227.2 1.3 fusion.59
  229.9 1.3 fusion.59
  232.5 1.3 fusion.59
  235.1 1.3 fusion.59
  237.8 1.3 fusion.59
  240.4 1.3 fusion.59
  245.6 1.3 fusion.59
  248.3 1.3 fusion.59
  253.5 1.3 fusion.59
  258.8 1.3 fusion.59
  260.5 2.7 convolution_convert_fusion
  263.2 4.6 %copy.73 = bf16[768,2048]{0,1:T(8,128)(2,1)} copy(bf16[768,2048]{1,0:T(8,128)(2,1)} %convolution_convert_fusion) | data formatting | bytes 6291456
  267.8 82.1 %reduce-scatter.4.cloned.1.call-done = bf16[128,768]{1,0:T(8,128)(2,1)} async-done(((bf16[2048,768]{1,0:T(8,128)(2,1)}), bf16[128,768]{1,0:T(8,128)(2,1)}) %reduce-scatter.4.cloned.1.call-update) | async-done | bytes 196624
  349.9 1.7 copy.74
  (145 shorter events, 34.4 us)
Async XLA Ops:
  6.5 254.0 %copy-start = (bf16[128,2048]{1,0:T(8,128)(2,1)S(1)}, bf16[128,2048]{1,0:T(8,128)(2,1)}, u32[]{:S(2)}) copy-start(bf16[128,2048]{1,0:T(8,128)(2,1)} %param.12) | copy-start | bytes 1572868
  6.5 61.5 %all-gather.3.cloned.1.call-start = ((), (), s32[]{:S(2)}) async-start(), calls=%async_computation.1 | async-start | bytes 3342336 | tf_op jit(solution)/shard_map/all_gather | solution.py:30
  7.3 210.9 %all-gather.5.cloned.1.call-start = ((), (), s32[]{:S(2)}) async-start(), calls=%async_computation.2 | async-start | bytes 6684672 | tf_op jit(solution)/shard_map/all_gather | solution.py:66
  9.0 61.7 %copy-start.4 = (f32[2048]{0:T(1024)S(1)}, f32[2048]{0:T(1024)}, u32[]{:S(2)}) copy-start(f32[2048]{0:T(1024)} %param.10) | copy-start | bytes 24580
  68.0 2.8 copy-start.1
  78.2 1.9 copy-start.2
  78.2 2.0 copy-start.3
  79.4 270.5 %reduce-scatter.4.cloned.1.call-start = ((), (), s32[]{:S(2)}) async-start(), calls=%async_computation.3 | async-start | bytes 3342336
Sparse Core Ops, SparseCore 0:
  9.9 58.0 all-gather.2
  79.6 138.5 all-gather.4
  268.0 81.9 reduce-scatter.3
where the time goes:
time: 362 us; the launch traced here: 358 us
  waiting for transfers between devices  275 us (76%)
  matrix products  46.5 us (13%)
  local copies, waits for them, and re-layouts  14.9 us (4%)
  between operations  14 us (4%)
  other arithmetic  6.41 us (2%)
    all_gather x1, waiting for transfers between devices, on_device(): kv_piece = lax.all_gather(kv_pairs, 'camtime', axis=0, tiled=True)  133 us
    unnamed x4, waiting for transfers between devices  82.8 us
    all_gather x1, waiting for transfers between devices, on_device(): lax.all_gather(tokens, 'heads', axis=1, tiled=True).astype(jnp.float32)  59 us
    dot_general x16, matrix products, one(): jnp.einsum('fchpq,cqhe->fchpe', expo_time.astype(jnp.bfloat16), pair[1],...  20 us
    dot_general x16, matrix products, one(): jnp.einsum('fcphe,cqhe->fchpq', query, pair[0], preferred_element_type=jn...  19.1 us
    unnamed x15, local copies, waits for them, and re-layouts  9.71 us
  transfers between devices with their start and end apart: 3, of which 3 were waited for; matrix products, arithmetic and copies ran while one was open for 2% of the time, Pallas kernels for 0%

commit v1 on v0

v1 whole, which is shorter than its diff:
```python
import functools

import jax
import jax.numpy as jnp
from jax import lax
from jax.experimental import pallas as pl
from jax.experimental.pallas import tpu as pltpu
from jax.sharding import PartitionSpec as P

HEADS = 16
PLANES = 8
GROUP = 3
DEPTH = 128
PATCH = 128
WIDTH = HEADS * DEPTH
ROWS = 2 * PATCH
MASKED = -3e38
LOWEST = -1e30
LOG2E = 1.4426950408889634
UP = (4, 4, 3)
DOWN = (3, 3, 4)
AG_SENDS = 15


def unit_rows(raw):
    return raw * lax.rsqrt(jnp.mean(raw * raw, axis=-1, keepdims=True) + 1e-06)


def kernel(
    x_ref, gain_ref, w_hbm, e_hbm, sharp_ref, adj_ref, allowed_ref, out_ref,
    xg, mg, kv, kc, w_ref, e_ref, e_all, scaled, qt, top_ref, total_ref, acc_ref, ostage, oland,
    x_recv, x_send, m_recv, m_send, a_recv, a_send, up_recv, up_send, dn_recv, dn_send,
    c_recv, c_send, e_recv, e_send, o_recv, o_send, load_sem,
):
    t = lax.axis_index("camtime")
    h = lax.axis_index("heads")
    z, j = t // 2, t % 2
    a, y, p = h // 8, (h // 2) % 4, h % 2

    def head(a_, y_, p_):
        return a_ * 8 + y_ * 2 + p_

    y_up, y_dn, y_far = (y + 1) % 4, (y + 3) % 4, (y + 2) % 4
    h_x, h_up, h_dn, h_sib = head(1 - a, y, p), head(a, y_up, p), head(a, y_dn, p), head(a, y, 1 - p)
    t_x = z * 2 + 1 - j
    t_up = ((z + 1) % PLANES) * 2 + j
    t_dn = ((z + PLANES - 1) % PLANES) * 2 + j
    mine = GROUP * j
    theirs = GROUP * (1 - j)

    def remote(src, dst, send, recv, heads=None, camtime=None):
        return pltpu.make_async_remote_copy(
            src_ref=src, dst_ref=dst, send_sem=send, recv_sem=recv,
            device_id={"camtime": t if camtime is None else camtime, "heads": h if heads is None else heads},
            device_id_type=pl.DeviceIdType.MESH,
        )

    def arrived(ref, sem):
        pltpu.make_async_copy(ref, ref, sem).wait()

    barrier = pltpu.get_barrier_semaphore()

    def greet(camtime, heads):
        pl.semaphore_signal(
            barrier, inc=1, device_id={"camtime": camtime, "heads": heads}, device_id_type=pl.DeviceIdType.MESH
        )

    for other in range(1, HEADS):
        greet(t, (h + other) % HEADS)
    greet(t_x, h)
    greet(t_up, h)
    greet(t_dn, h)

    w_load = pltpu.make_async_copy(w_hbm, w_ref, load_sem.at[0])
    w_load.start()
    e_load = pltpu.make_async_copy(e_hbm, e_ref, load_sem.at[1])
    e_load.start()
    for c in range(GROUP):
        xg[c, h, j] = x_ref[mine + c]
        top_ref[c] = jnp.full((1, ROWS), LOWEST, jnp.float32)
        total_ref[c] = jnp.zeros((1, ROWS), jnp.float32)
        acc_ref[c] = jnp.zeros((DEPTH, ROWS), jnp.float32)
    pl.semaphore_wait(barrier, HEADS + 2)

    swaps = []
    for c in range(GROUP):
        copy = remote(x_ref.at[theirs + c], xg.at[c, h, j], a_send.at[c], a_recv.at[c], camtime=t_x)
        copy.start()
        swaps.append(copy)

    class Gather:
        def __init__(self, buf, recv, send):
            self.buf, self.recv, self.send, self.sent = buf, recv, send, [[] for _ in range(GROUP)]

        def push(self, c, slot, to):
            copy = remote(
                self.buf.at[c, slot], self.buf.at[c, slot], self.send.at[c, len(self.sent[c])],
                self.recv.at[c, slot], heads=to,
            )
            copy.start()
            self.sent[c].append(copy)

        def take(self, c, slot):
            arrived(self.buf.at[c, slot], self.recv.at[c, slot])

        def own(self, c):
            for to in (h_x, h_up, h_dn, h_sib):
                self.push(c, h, to)

        def across(self, c):
            self.take(c, h_x)
            for to in (h_up, h_dn, h_sib):
                self.push(c, h_x, to)

        def near(self, c):
            slot = head(a, y_dn, p)
            self.take(c, slot)
            self.push(c, slot, h_up)
            self.push(c, slot, h_sib)
            slot = head(a, y_up, p)
            self.take(c, slot)
            self.push(c, slot, h_sib)
            slot = head(1 - a, y_up, p)
            self.take(c, slot)
            self.push(c, slot, h_dn)
            self.push(c, slot, h_sib)
            slot = head(1 - a, y_dn, p)
            self.take(c, slot)
            self.push(c, slot, h_sib)

        def far(self, c):
            for a_ in (a, 1 - a):
                slot = head(a_, y_far, p)
                self.take(c, slot)
                self.push(c, slot, h_sib)

        def rest(self, c):
            for a_ in range(2):
                for y_ in range(4):
                    self.take(c, head(a_, y_, 1 - p))

    xs = Gather(xg, x_recv, x_send)
    ms = Gather(mg, m_recv, m_send)

    scale = sharp_ref[0] * (LOG2E / DEPTH**0.5)

    def up_copy(c, d):
        src = kc.at[mine + c] if d == 0 else kv.at[z - d, c]
        return remote(src, kv.at[z - d, c], up_send.at[c, d], up_recv.at[c, d], camtime=t_up)

    def dn_copy(c, hop):
        plane = (z + hop) % PLANES
        src = kc.at[mine + c] if hop == 0 else kv.at[plane, c]
        return remote(src, kv.at[plane, c], dn_send.at[c, hop], dn_recv.at[c, hop], camtime=t_dn)

    def cross_copy(c):
        return remote(kc.at[mine + c], kc.at[mine + c], c_send.at[c], c_recv.at[c], camtime=t_x)

    def project(c):
        squares = jnp.zeros((ROWS, DEPTH), jnp.float32)
        for d in range(HEADS):
            wide = xg[c, d].reshape(ROWS, DEPTH).astype(jnp.float32)
            squares = squares + wide * wide
            scaled[:, d * DEPTH:(d + 1) * DEPTH] = (wide * gain_ref[d:d + 1, :]).astype(jnp.bfloat16)
        inv_rms = lax.rsqrt(jnp.sum(squares, axis=1, keepdims=True) / WIDTH + 1e-06)
        raw = jnp.dot(scaled[...], w_ref[...], preferred_element_type=jnp.float32) * inv_rms
        query = unit_rows(raw[:, :DEPTH])
        key = unit_rows(raw[:, DEPTH:2 * DEPTH]).astype(jnp.bfloat16)
        value = raw[:, 2 * DEPTH:]
        qt[c] = query.T.astype(jnp.bfloat16)
        for f in range(2):
            kc[mine + c, f] = key[f * PATCH:(f + 1) * PATCH]
            kc[mine + c, 2 + f] = value[f * PATCH:(f + 1) * PATCH].T.astype(jnp.bfloat16)

        @pl.when(z < PLANES - 1)
        def _():
            up_copy(c, 0).start()

        @pl.when(z < DOWN[c])
        def _():
            dn_copy(c, 0).start()

        cross_copy(c).start()

    def bias(plane, f, c):
        return jnp.where(allowed_ref[2 * plane + f, mine + c] == 1, 0.0, MASKED).astype(jnp.float32)

    def fold(c, score, values, lanes):
        before = top_ref[c, :, lanes]
        top = jnp.maximum(before, jnp.max(score, axis=0, keepdims=True))
        expo = jnp.exp2(score - top)
        rescale = jnp.exp2(before - top)
        top_ref[c, :, lanes] = top
        total_ref[c, :, lanes] = total_ref[c, :, lanes] * rescale + jnp.sum(expo, axis=0, keepdims=True)
        acc_ref[c, :, lanes] = acc_ref[c, :, lanes] * rescale + jnp.dot(
            values, expo.astype(jnp.bfloat16), preferred_element_type=jnp.float32
        )

    def attend(c, plane):
        score = jnp.dot(kv[plane, c, 0:2].reshape(ROWS, DEPTH), qt[c], preferred_element_type=jnp.float32) * scale
        score = jnp.concatenate(
            [score[:PATCH] + bias(plane, 0, c), score[PATCH:] + bias(plane, 1, c)], axis=0
        )
        values = jnp.concatenate([kv[plane, c, 2], kv[plane, c, 3]], axis=1)
        fold(c, score, values, slice(0, ROWS))

    def attend_cross(c):
        cam = mine + c
        for f in range(2):
            lanes = slice(f * PATCH, (f + 1) * PATCH)
            near = [cam, adj_ref[cam, 0], adj_ref[cam, 1]]
            keys = [kc[n, f] for n in near]
            values = [kc[n, 2 + f] for n in near]
            if f == 1:
                keys.append(kc[cam, 0])
                values.append(kc[cam, 2])
            score = jnp.dot(jnp.concatenate(keys, axis=0), qt[c, :, lanes], preferred_element_type=jnp.float32) * scale
            if f == 1:
                score = jnp.concatenate([score[:3 * PATCH], score[3 * PATCH:] + bias(z, 0, c)], axis=0)
            fold(c, score, jnp.concatenate(values, axis=1), lanes)

    def step_up(c, d):
        @pl.when(z >= d)
        def _():
            arrived(kv.at[z - d, c], up_recv.at[c, d - 1])
            if d < UP[c]:
                @pl.when(z < PLANES - 1)
                def _():
                    up_copy(c, d).start()
            attend(c, z - d)

    def step_dn(c, hop):
        plane = (z + hop) % PLANES

        @pl.when(plane < DOWN[c])
        def _():
            arrived(kv.at[plane, c], dn_recv.at[c, hop - 1])
            if hop < DOWN[c]:
                dn_copy(c, hop).start()

            @pl.when(plane < z)
            def _():
                attend(c, plane)

    def finish(c):
        mixed = acc_ref[c] / total_ref[c]
        mg[c, h] = mixed.T.astype(jnp.bfloat16).reshape(2, PATCH, DEPTH)
        ms.own(c)

    def out_copy(c):
        return remote(ostage.at[c, 1 - j], oland.at[c], o_send.at[c], o_recv.at[c], camtime=t_x)

    def project_out(c):
        summed = jnp.zeros((ROWS, DEPTH), jnp.float32)
        for d in range(HEADS):
            part = jnp.dot(mg[c, d].reshape(ROWS, DEPTH), e_all[d], preferred_element_type=jnp.float32)
            summed = summed + part.astype(jnp.bfloat16).astype(jnp.float32)
        ostage[c] = summed.astype(jnp.bfloat16).reshape(2, PATCH, DEPTH)
        out_copy(c).start()
        out_ref[mine + c] = ostage[c, j]

    for c in range(GROUP):
        arrived(xg.at[c, h, 1 - j], a_recv.at[c])
        xs.own(c)
    for c in range(GROUP):
        xs.across(c)
    w_load.wait()

    xs.near(0)
    xs.far(0)
    xs.rest(0)
    project(0)
    xs.near(1)
    xs.far(1)
    xs.rest(1)
    project(1)
    step_up(0, 1)
    step_dn(0, 1)
    xs.near(2)
    xs.far(2)
    xs.rest(2)
    project(2)

    e_load.wait()
    e_sends = []
    for other in range(1, HEADS):
        to = (h + other) % HEADS
        copy = remote(
            e_ref.at[:, pl.ds(pl.multiple_of(to * DEPTH, DEPTH), DEPTH)], e_all.at[h],
            e_send.at[other], e_recv.at[h], heads=to,
        )
        copy.start()
        e_sends.append(copy)
    e_all[h] = e_ref[:, pl.ds(pl.multiple_of(h * DEPTH, DEPTH), DEPTH)]

    step_up(1, 1)
    step_dn(1, 1)
    step_up(0, 2)
    step_dn(0, 2)
    step_up(2, 1)
    step_dn(2, 1)
    step_up(0, 3)
    step_dn(0, 3)
    step_up(1, 2)
    step_dn(1, 2)
    for c in range(GROUP):
        arrived(kc.at[theirs + c], c_recv.at[c])
    attend_cross(0)
    step_up(0, 4)
    finish(0)
    step_up(1, 3)
    step_dn(1, 3)
    step_up(2, 2)
    step_dn(2, 2)
    ms.across(0)
    attend_cross(1)
    step_up(1, 4)
    finish(1)
    ms.near(0)
    ms.across(1)
    step_up(2, 3)
    step_dn(2, 3)
    attend_cross(2)
    step_dn(2, 4)
    finish(2)
    ms.far(0)
    ms.near(1)
    ms.across(2)
    ms.rest(0)
    for other in range(1, HEADS):
        slot = (h + other) % HEADS
        arrived(e_all.at[slot], e_recv.at[slot])
    project_out(0)
    ms.far(1)
    ms.near(2)
    ms.rest(1)
    project_out(1)
    ms.far(2)
    ms.rest(2)
    project_out(2)
    for c in range(GROUP):
        arrived(oland.at[c], o_recv.at[c])
        out_ref[theirs + c] = oland[c]

    for copy in swaps + e_sends:
        copy.wait_send()
    for c in range(GROUP):
        for copy in xs.sent[c] + ms.sent[c]:
            copy.wait_send()
        cross_copy(c).wait_send()
        out_copy(c).wait_send()
        for d in range(UP[c]):
            @pl.when((z >= d) & (z < PLANES - 1))
            def _():
                up_copy(c, d).wait_send()
        for hop in range(DOWN[c]):
            @pl.when((z + hop) % PLANES < DOWN[c])
            def _():
                dn_copy(c, hop).wait_send()


def on_device(
    hidden_patch_vectors,
    entry_rms_multiplier,
    lookup_projection_matrix,
    exit_projection_matrix,
    probe_sharpness,
    adjacent_camera_pairs,
    prior_frame_allowed,
):
    frames, cams, patches, local_width = hidden_patch_vectors.shape
    vmem = pl.BlockSpec(memory_space=pltpu.VMEM)
    smem = pl.BlockSpec(memory_space=pltpu.SMEM)
    hbm = pl.BlockSpec(memory_space=pl.ANY)
    dma = pltpu.SemaphoreType.DMA
    bf16, f32 = jnp.bfloat16, jnp.float32
    result = pl.pallas_call(
        kernel,
        out_shape=jax.ShapeDtypeStruct((cams, patches, local_width), bf16),
        in_specs=[vmem, vmem, hbm, hbm, smem, smem, smem],
        out_specs=vmem,
        scratch_shapes=[
            pltpu.VMEM((GROUP, HEADS, 2, PATCH, DEPTH), bf16),
            pltpu.VMEM((GROUP, HEADS, 2, PATCH, DEPTH), bf16),
            pltpu.VMEM((PLANES, GROUP, 4, PATCH, DEPTH), bf16),
            pltpu.VMEM((2 * GROUP, 4, PATCH, DEPTH), bf16),
            pltpu.VMEM((WIDTH, 3 * DEPTH), bf16),
            pltpu.VMEM((DEPTH, WIDTH), bf16),
            pltpu.VMEM((HEADS, DEPTH, DEPTH), bf16),
            pltpu.VMEM((ROWS, WIDTH), bf16),
            pltpu.VMEM((GROUP, DEPTH, ROWS), bf16),
            pltpu.VMEM((GROUP, 1, ROWS), f32),
            pltpu.VMEM((GROUP, 1, ROWS), f32),
            pltpu.VMEM((GROUP, DEPTH, ROWS), f32),
            pltpu.VMEM((GROUP, 2, PATCH, DEPTH), bf16),
            pltpu.VMEM((GROUP, PATCH, DEPTH), bf16),
            dma((GROUP, HEADS)), dma((GROUP, AG_SENDS)),
            dma((GROUP, HEADS)), dma((GROUP, AG_SENDS)),
            dma((GROUP,)), dma((GROUP,)),
            dma((GROUP, 4)), dma((GROUP, 4)),
            dma((GROUP, 4)), dma((GROUP, 4)),
            dma((GROUP,)), dma((GROUP,)),
            dma((HEADS,)), dma((HEADS,)),
            dma((GROUP,)), dma((GROUP,)),
            dma((2,)),
        ],
        compiler_params=pltpu.CompilerParams(
            collective_id=0, has_side_effects=True, vmem_limit_bytes=48 * 1024 * 1024
        ),
    )(
        hidden_patch_vectors.reshape(cams, patches, local_width),
        entry_rms_multiplier.reshape(HEADS, DEPTH),
        lookup_projection_matrix.reshape(WIDTH, 3 * DEPTH),
        exit_projection_matrix,
        probe_sharpness,
        adjacent_camera_pairs,
        prior_frame_allowed,
    )
    return result.reshape(frames, cams, patches, local_width)


def solution(mesh):
    placed = (
        P("camtime", None, None, "heads"),
        P(),
        P(None, None, "heads"),
        P("heads", None),
        P("heads"),
        P(),
        P(),
    )
    return jax.shard_map(
        on_device,
        mesh=mesh,
        in_specs=placed,
        out_specs=P("camtime", None, None, "heads"),
        check_vma=False,
    )
```

time: 362 us -> 91.3 us (0.25)
  waiting for transfers between devices: 275 us -> 0 us
  Pallas kernels: 0 us -> 84.5 us
  matrix products: 46.5 us -> 0 us
  between operations: 14 us -> 0.72 us
  local copies, waits for them, and re-layouts: 14.9 us -> 5.48 us
  other arithmetic: 6.41 us -> 0 us
    all_gather x2 -> x0, waiting for transfers between devices: 192 us -> none  [the longest x1 133 us: on_device(): kv_piece = lax.all_gather(kv_pairs, 'camtime', axis=0, tiled=True)]
    pallas_call x0 -> x1, Pallas kernels: none -> 84.5 us  [on_device(): pl.pallas_call(kernel, out_shape=jax.ShapeDtypeStruct((cams, patches, loc...]
    unnamed x4 -> x0, waiting for transfers between devices: 82.8 us -> none
    dot_general x38 -> x0, matrix products: 46.5 us -> none  [the longest x16 20 us: one(): jnp.einsum('fchpq,cqhe->fchpe', expo_time.astype(jnp.bfloat16), pair[1],...]
    unnamed x15 -> x14, local copies, waits for them, and re-layouts: 9.71 us -> 3.53 us
    reduce_sum x20 -> x0, other arithmetic: 4.6 us -> none  [the longest x1 2.72 us: on_device(): accum, squares = (accum, jnp.sum(wide * wide, axis=1))]
  transfers between devices with their start and end apart: 3 -> 0, of which waited for: 3 -> 0; matrix products, arithmetic and copies ran while one was open for 2% -> 0% of each run, Pallas kernels for 0% -> 0%
where the time goes in v1:
time: 91.3 us; the launch traced here: 90.7 us
  Pallas kernels  84.5 us (93%)
  local copies, waits for them, and re-layouts  5.48 us (6%)
    pallas_call x1, Pallas kernels, on_device(): pl.pallas_call(kernel, out_shape=jax.ShapeDtypeStruct((cams, patches, loc...  84.5 us
    unnamed x14, local copies, waits for them, and re-layouts  3.53 us
    reshape x1, local copies, waits for them, and re-layouts, on_device(): lookup_projection_matrix.reshape(WIDTH, 3 * DEPTH)  1.95 us

profile of v1, /device:TPU:193, one launch (start us, length us, event | category | flops | bytes accessed | tf_op | source)
XLA Modules:
  0.0 90.7 jit_solution(10875377135566151467)
XLA Ops:
  0.0 2.7 %copy.11 = bf16[2048,3,128]{0,2,1:T(8,128)(2,1)} copy(bf16[2048,3,128]{2,0,1:T(8,128)(2,1)} %param.9) | data formatting | bytes 3145728 | tf_op args[2]
  2.7 0.0 copy-start.3
  2.7 0.0 copy-start.4
  2.7 0.0 copy-start
  2.7 0.0 copy-start.1
  2.7 0.0 copy-start.2
  2.7 1.9 %copy.12.w_hbm = bf16[2048,384]{1,0:T(8,128)(2,1)S(1)} copy(bf16[2048,384]{0,1:T(8,128)(2,1)} %bitcast.7) | data formatting | bytes 3145728 | tf_op jit(solution)/shard_map/reshape | solution.py:413
  4.6 0.0 copy-done.3
  4.6 0.1 copy.14.allowed_ref
  4.7 0.0 copy-done.4
  4.7 0.1 copy.13.adj_ref
  5.5 0.0 copy-done
  5.5 0.0 copy-done.1
  5.5 0.0 copy-done.2
  5.5 84.5 %shard_map.73 = bf16[6,128,128]{2,1,0:T(8,128)(2,1)S(1)} custom-call(bf16[6,128,128]{2,1,0:T(8,128)(2,1)S(1)} %bitcast.5, f32[16,128]{1,0:T(8,128)S(1)} %bitcast.6, bf16[2048,384]{1,0:T(8,128)(2,1)S(1)} %copy.12.w_hbm, bf16[128,2048]{1,0:T(8,128)(2,1)S(1)} %copy-done, f32[1]{0:T(128)S(6)} %copy.16.sharp_ref, s32[6,2]{1,0:T(8,128)S(1)} %copy.13.adj_ref, ...), custom_call_target="tpu_custom_call" | custom-call | tf_op jit(solution)/shard_map/pallas_call | solution.py:377
  90.0 0.7 copy.17
Async XLA Ops:
  2.7 2.0 %copy-start.3 = (s32[16,6]{0,1:T(8,128)S(1)}, s32[16,6]{0,1:T(8,128)}, u32[]{:S(2)}) copy-start(s32[16,6]{0,1:T(8,128)} %param.13) | copy-start | bytes 1156
  2.7 2.1 %copy-start.4 = (s32[6,2]{0,1:T(2,128)S(1)}, s32[6,2]{0,1:T(2,128)}, u32[]{:S(2)}) copy-start(s32[6,2]{0,1:T(2,128)} %param.12) | copy-start | bytes 148
  2.7 2.8 %copy-start = (bf16[128,2048]{1,0:T(8,128)(2,1)S(1)}, bf16[128,2048]{1,0:T(8,128)(2,1)}, u32[]{:S(2)}) copy-start(bf16[128,2048]{1,0:T(8,128)(2,1)} %e_hbm.1) | copy-start | bytes 1572868
  2.7 2.8 %copy-start.1 = (bf16[1,6,128,128]{3,2,1,0:T(8,128)(2,1)S(1)}, bf16[1,6,128,128]{3,2,1,0:T(8,128)(2,1)}, u32[]{:S(2)}) copy-start(bf16[1,6,128,128]{3,2,1,0:T(8,128)(2,1)} %param.7) | copy-start | bytes 589828
  2.7 2.8 %copy-start.2 = (f32[2048]{0:T(1024)S(1)}, f32[2048]{0:T(1024)}, u32[]{:S(2)}) copy-start(f32[2048]{0:T(1024)} %param.8) | copy-start | bytes 24580

commit v2 on v1

v2 whole, which is shorter than its diff:
```python
import jax
import jax.numpy as jnp
from jax import lax
from jax.experimental import pallas as pl
from jax.experimental.pallas import tpu as pltpu
from jax.sharding import PartitionSpec as P

HEADS = 16
ROW = 4
PLANES = 8
GROUP = 3
DEPTH = 128
PATCH = 128
WIDTH = HEADS * DEPTH
ROWS = 2 * PATCH
MASKED = -3e38
LOWEST = -1e30
LOG2E = 1.4426950408889634
UP = (4, 4, 3)
DOWN = (3, 3, 4)


def unit_rows(raw):
    return raw * lax.rsqrt(jnp.mean(raw * raw, axis=-1, keepdims=True) + 1e-06)


def kernel(
    x_hbm, gain_ref, w_hbm, e_hbm, sharp_ref, adj_ref, allowed_ref, out_ref,
    xg, mg, mstage, kv, kc, w_ref, e_ref, e_all, scaled, raw_ref, qt, top_ref, total_ref, acc_ref,
    x_recv, x_sib, x_send, x_sib_send, m_recv, m_sib, m_send, m_sib_send,
    up_recv, up_send, dn_recv, dn_send, c_recv, c_send, e_recv, e_send, load_sem,
):
    t = lax.axis_index("camtime")
    h = lax.axis_index("heads")
    z, j = t // 2, t % 2
    a, y, p = h // 8, (h // 2) % ROW, h % 2

    def head(a_, y_, p_):
        return a_ * 8 + y_ * 2 + p_

    rows = [y, (y + 1) % ROW, (y + 3) % ROW, (y + 2) % ROW]
    h_sib = head(a, y, 1 - p)
    t_x = z * 2 + 1 - j
    t_up = ((z + 1) % PLANES) * 2 + j
    t_dn = ((z + PLANES - 1) % PLANES) * 2 + j
    mine = GROUP * j
    theirs = GROUP * (1 - j)

    def remote(src, dst, send, recv, heads=None, camtime=None):
        return pltpu.make_async_remote_copy(
            src_ref=src, dst_ref=dst, send_sem=send, recv_sem=recv,
            device_id={"camtime": t if camtime is None else camtime, "heads": h if heads is None else heads},
            device_id_type=pl.DeviceIdType.MESH,
        )

    def arrived(ref, sem):
        pltpu.make_async_copy(ref, ref, sem).wait()

    barrier = pltpu.get_barrier_semaphore()

    def greet(camtime, heads):
        pl.semaphore_signal(
            barrier, inc=1, device_id={"camtime": camtime, "heads": heads}, device_id_type=pl.DeviceIdType.MESH
        )

    for other in range(1, HEADS):
        greet(t, (h + other) % HEADS)
    for other in range(0, HEADS, 2):
        greet(t_x, (h + other) % HEADS)
    greet(t_up, h)
    greet(t_dn, h)

    def x_slot(c, p_, y_, a_, f):
        return ((c * 2 + p_) * ROW + y_) * 4 + a_ * 2 + f

    def m_slot(cam, p_, y_, a_):
        return ((cam * 2 + p_) * ROW + y_) * 2 + a_

    for c in range(GROUP):
        pltpu.make_async_copy(x_hbm.at[mine + c], xg.at[x_slot(c, p, y, a, j)], x_recv.at[c, y]).start()
    w_loads = []
    for i in range(3):
        load = pltpu.make_async_copy(w_hbm.at[i], w_ref.at[:, i * DEPTH:(i + 1) * DEPTH], load_sem.at[i])
        load.start()
        w_loads.append(load)
    e_load = pltpu.make_async_copy(e_hbm, e_ref, load_sem.at[3])
    e_load.start()
    for c in range(GROUP):
        top_ref[c] = jnp.full((1, ROWS), LOWEST, jnp.float32)
        total_ref[c] = jnp.zeros((1, ROWS), jnp.float32)
        acc_ref[c] = jnp.zeros((DEPTH, ROWS), jnp.float32)
    pl.semaphore_wait(barrier, HEADS - 1 + HEADS // 2 + 2)

    chips = [(a_, y_) for y_ in rows for a_ in (1 - a, a)]

    def x_push(c):
        slot = x_slot(c, p, y, a, j)
        for n, (a_, y_) in enumerate(chips):
            remote(x_hbm.at[theirs + c], xg.at[slot], x_send.at[c], x_recv.at[c, y],
                   heads=head(a_, y_, p), camtime=t_x).start()
            if n != 1:
                remote(x_hbm.at[mine + c], xg.at[slot], x_send.at[c], x_recv.at[c, y],
                       heads=head(a_, y_, p)).start()

    def x_relay(c):
        for y_ in rows:
            row = xg.at[pl.ds(x_slot(c, p, y_, 0, 0), 4)]
            arrived(row, x_recv.at[c, y_])
            remote(row, row, x_sib_send.at[c], x_sib.at[c, y_], heads=h_sib).start()

    def x_sent(c):
        arrived(xg.at[pl.ds(0, 15)], x_send.at[c])
        arrived(xg.at[pl.ds(0, 16)], x_sib_send.at[c])

    scale = sharp_ref[0] * (LOG2E / DEPTH**0.5)

    def up_copy(c, d):
        src = kc.at[mine + c] if d == 0 else kv.at[z - d, c]
        return remote(src, kv.at[z - d, c], up_send.at[c, d], up_recv.at[c, d], camtime=t_up)

    def dn_copy(c, hop):
        plane = (z + hop) % PLANES
        src = kc.at[mine + c] if hop == 0 else kv.at[plane, c]
        return remote(src, kv.at[plane, c], dn_send.at[c, hop], dn_recv.at[c, hop], camtime=t_dn)

    def cross_copy(c):
        return remote(kc.at[mine + c], kc.at[mine + c], c_send.at[c], c_recv.at[c], camtime=t_x)

    def project(c):
        squares = jnp.zeros((ROWS, DEPTH), jnp.float32)
        for n, y_ in enumerate(rows):
            arrived(xg.at[pl.ds(x_slot(c, 1 - p, y_, 0, 0), 4)], x_sib.at[c, y_])
            for a_ in range(2):
                for p_ in range(2):
                    wide = xg[pl.ds(x_slot(c, p_, y_, a_, 0), 2)].reshape(ROWS, DEPTH).astype(jnp.float32)
                    squares = squares + wide * wide
                    scaled[:, (a_ * 2 + p_) * DEPTH:(a_ * 2 + p_ + 1) * DEPTH] = (
                        wide * gain_ref[head(a_, y_, p_)]
                    ).astype(jnp.bfloat16)
            part = jnp.zeros((ROWS, 3 * DEPTH), jnp.float32) if n == 0 else raw_ref[...]
            for a_ in range(2):
                part = part + jnp.dot(
                    scaled[:, a_ * 2 * DEPTH:(a_ + 1) * 2 * DEPTH],
                    w_ref[pl.ds(pl.multiple_of(head(a_, y_, 0) * DEPTH, 2 * DEPTH), 2 * DEPTH), :],
                    preferred_element_type=jnp.float32,
                )
            raw_ref[...] = part
        inv_rms = lax.rsqrt(jnp.sum(squares, axis=1, keepdims=True) / WIDTH + 1e-06)
        raw = raw_ref[...] * inv_rms
        key = unit_rows(raw[:, DEPTH:2 * DEPTH]).astype(jnp.bfloat16)
        value = raw[:, 2 * DEPTH:]
        for f in range(2):
            kc[mine + c, f] = key[f * PATCH:(f + 1) * PATCH]
            kc[mine + c, 2 + f] = value[f * PATCH:(f + 1) * PATCH].T.astype(jnp.bfloat16)

        @pl.when(z < PLANES - 1)
        def _():
            up_copy(c, 0).start()

        @pl.when(z < DOWN[c])
        def _():
            dn_copy(c, 0).start()

        cross_copy(c).start()
        qt[c] = unit_rows(raw[:, :DEPTH]).T.astype(jnp.bfloat16)

    def bias(plane, f, c):
        return jnp.where(allowed_ref[mine + c, 2 * plane + f] == 1, 0.0, MASKED).astype(jnp.float32)

    def fold(c, score, values, lanes):
        before = top_ref[c, :, lanes]
        top = jnp.maximum(before, jnp.max(score, axis=0, keepdims=True))
        expo = jnp.exp2(score - top)
        rescale = jnp.exp2(before - top)
        top_ref[c, :, lanes] = top
        total_ref[c, :, lanes] = total_ref[c, :, lanes] * rescale + jnp.sum(expo, axis=0, keepdims=True)
        acc_ref[c, :, lanes] = acc_ref[c, :, lanes] * rescale + jnp.dot(
            values, expo.astype(jnp.bfloat16), preferred_element_type=jnp.float32
        )

    def attend(c, plane):
        score = jnp.dot(kv[plane, c, 0:2].reshape(ROWS, DEPTH), qt[c], preferred_element_type=jnp.float32) * scale
        score = jnp.concatenate(
            [score[:PATCH] + bias(plane, 0, c), score[PATCH:] + bias(plane, 1, c)], axis=0
        )
        values = jnp.concatenate([kv[plane, c, 2], kv[plane, c, 3]], axis=1)
        fold(c, score, values, slice(0, ROWS))

    def attend_cross(c):
        if c == 0:
            for other in range(GROUP):
                arrived(kc.at[theirs + other], c_recv.at[other])
        cam = mine + c
        for f in range(2):
            lanes = slice(f * PATCH, (f + 1) * PATCH)
            near = [cam, adj_ref[0, cam], adj_ref[1, cam]]
            keys = [kc[n, f] for n in near]
            values = [kc[n, 2 + f] for n in near]
            if f == 1:
                keys.append(kc[cam, 0])
                values.append(kc[cam, 2])
            score = jnp.dot(jnp.concatenate(keys, axis=0), qt[c, :, lanes], preferred_element_type=jnp.float32) * scale
            if f == 1:
                score = jnp.concatenate([score[:3 * PATCH], score[3 * PATCH:] + bias(z, 0, c)], axis=0)
            fold(c, score, jnp.concatenate(values, axis=1), lanes)

    def step_up(c, d):
        @pl.when(z >= d)
        def _():
            arrived(kv.at[z - d, c], up_recv.at[c, d - 1])
            if d < UP[c]:
                @pl.when(z < PLANES - 1)
                def _():
                    up_copy(c, d).start()
            attend(c, z - d)

    def step_dn(c, hop):
        plane = (z + hop) % PLANES

        @pl.when(plane < DOWN[c])
        def _():
            arrived(kv.at[plane, c], dn_recv.at[c, hop - 1])
            if hop < DOWN[c]:
                dn_copy(c, hop).start()

            @pl.when(plane < z)
            def _():
                attend(c, plane)

    def m_push(c):
        mixed = (acc_ref[c] / total_ref[c]).T.astype(jnp.bfloat16).reshape(2, PATCH, DEPTH)
        mstage[c] = mixed
        cam = mine + c
        slot = m_slot(cam, p, y, a)
        for n, (a_, y_) in enumerate(chips):
            remote(mstage.at[c, 1 - j], mg.at[slot], m_send.at[c], m_recv.at[cam, y],
                   heads=head(a_, y_, p), camtime=t_x).start()
            if n != 1:
                remote(mstage.at[c, j], mg.at[slot], m_send.at[c], m_recv.at[cam, y],
                       heads=head(a_, y_, p)).start()
        mg[slot] = mstage[c, j]

    def m_relay(c):
        for n, y_ in enumerate(rows):
            for side, cam in enumerate((mine + c, theirs + c)):
                row = mg.at[pl.ds(m_slot(cam, p, y_, 0), 2)]
                if n == 0 and side == 0:
                    arrived(mg.at[pl.ds(m_slot(cam, p, y_, 0), 1)], m_recv.at[cam, y_])
                else:
                    arrived(row, m_recv.at[cam, y_])
                remote(row, row, m_sib_send.at[c], m_sib.at[cam, y_], heads=h_sib).start()

    def m_sent(c):
        arrived(xg.at[pl.ds(0, 15)], m_send.at[c])
        arrived(xg.at[pl.ds(0, 16)], m_sib_send.at[c])

    def project_out(c):
        summed = jnp.zeros((ROWS, DEPTH), jnp.float32)
        cams = (mine + c, theirs + c)
        for y_ in rows:
            for cam in cams:
                arrived(mg.at[pl.ds(m_slot(cam, 1 - p, y_, 0), 2)], m_sib.at[cam, y_])
            for a_ in range(2):
                for p_ in range(2):
                    mixed = jnp.concatenate([mg[m_slot(cam, p_, y_, a_)] for cam in cams], axis=0)
                    part = jnp.dot(mixed, e_all[head(a_, y_, p_)], preferred_element_type=jnp.float32)
                    summed = summed + part.astype(jnp.bfloat16).astype(jnp.float32)
        for n, cam in enumerate(cams):
            out_ref[cam] = summed[n * PATCH:(n + 1) * PATCH].astype(jnp.bfloat16)

    for c in range(GROUP):
        x_push(c)
    x_relay(0)
    for load in w_loads:
        load.wait()
    project(0)
    x_relay(1)
    step_up(0, 1)
    step_dn(0, 1)
    project(1)
    x_relay(2)
    step_up(0, 2)
    step_dn(0, 2)
    project(2)

    e_load.wait()
    e_sends = []
    for other in range(1, HEADS):
        to = (h + other) % HEADS
        copy = remote(
            e_ref.at[:, pl.ds(pl.multiple_of(to * DEPTH, DEPTH), DEPTH)], e_all.at[h],
            e_send.at[other], e_recv.at[h], heads=to,
        )
        copy.start()
        e_sends.append(copy)
    e_all[h] = e_ref[:, pl.ds(pl.multiple_of(h * DEPTH, DEPTH), DEPTH)]

    step_up(1, 1)
    step_dn(1, 1)
    step_up(0, 3)
    step_dn(0, 3)
    step_up(1, 2)
    step_dn(1, 2)
    step_up(2, 1)
    step_dn(2, 1)
    attend_cross(0)
    step_up(0, 4)
    m_push(0)
    attend_cross(1)
    step_up(1, 3)
    step_dn(1, 3)
    step_up(2, 2)
    step_dn(2, 2)
    step_up(1, 4)
    m_push(1)
    attend_cross(2)
    m_relay(0)
    step_up(2, 3)
    step_dn(2, 3)
    step_dn(2, 4)
    m_push(2)
    for other in range(1, HEADS):
        slot = (h + other) % HEADS
        arrived(e_all.at[slot], e_recv.at[slot])
    project_out(0)
    m_relay(1)
    project_out(1)
    m_relay(2)
    project_out(2)

    for copy in e_sends:
        copy.wait_send()
    for c in range(GROUP):
        x_sent(c)
        m_sent(c)
        cross_copy(c).wait_send()
        for d in range(UP[c]):
            @pl.when((z >= d) & (z < PLANES - 1))
            def _():
                up_copy(c, d).wait_send()
        for hop in range(DOWN[c]):
            @pl.when((z + hop) % PLANES < DOWN[c])
            def _():
                dn_copy(c, hop).wait_send()


def on_device(
    hidden_patch_vectors,
    entry_rms_multiplier,
    lookup_projection_matrix,
    exit_projection_matrix,
    probe_sharpness,
    adjacent_camera_pairs,
    prior_frame_allowed,
):
    frames, cams, patches, local_width = hidden_patch_vectors.shape
    vmem = pl.BlockSpec(memory_space=pltpu.VMEM)
    smem = pl.BlockSpec(memory_space=pltpu.SMEM)
    hbm = pl.BlockSpec(memory_space=pl.ANY)
    dma = pltpu.SemaphoreType.DMA
    bf16, f32 = jnp.bfloat16, jnp.float32
    result = pl.pallas_call(
        kernel,
        out_shape=jax.ShapeDtypeStruct((cams, patches, local_width), bf16),
        in_specs=[hbm, vmem, hbm, hbm, smem, smem, smem],
        out_specs=vmem,
        scratch_shapes=[
            pltpu.VMEM((GROUP * HEADS * 2, PATCH, DEPTH), bf16),
            pltpu.VMEM((2 * GROUP * HEADS, PATCH, DEPTH), bf16),
            pltpu.VMEM((GROUP, 2, PATCH, DEPTH), bf16),
            pltpu.VMEM((PLANES, GROUP, 4, PATCH, DEPTH), bf16),
            pltpu.VMEM((2 * GROUP, 4, PATCH, DEPTH), bf16),
            pltpu.VMEM((WIDTH, 3 * DEPTH), bf16),
            pltpu.VMEM((DEPTH, WIDTH), bf16),
            pltpu.VMEM((HEADS, DEPTH, DEPTH), bf16),
            pltpu.VMEM((ROWS, 4 * DEPTH), bf16),
            pltpu.VMEM((ROWS, 3 * DEPTH), f32),
            pltpu.VMEM((GROUP, DEPTH, ROWS), bf16),
            pltpu.VMEM((GROUP, 1, ROWS), f32),
            pltpu.VMEM((GROUP, 1, ROWS), f32),
            pltpu.VMEM((GROUP, DEPTH, ROWS), f32),
            dma((GROUP, ROW)), dma((GROUP, ROW)), dma((GROUP,)), dma((GROUP,)),
            dma((2 * GROUP, ROW)), dma((2 * GROUP, ROW)), dma((GROUP,)), dma((GROUP,)),
            dma((GROUP, 4)), dma((GROUP, 4)),
            dma((GROUP, 4)), dma((GROUP, 4)),
            dma((GROUP,)), dma((GROUP,)),
            dma((HEADS,)), dma((HEADS,)),
            dma((4,)),
        ],
        compiler_params=pltpu.CompilerParams(
            collective_id=0, has_side_effects=True, vmem_limit_bytes=60 * 1024 * 1024
        ),
    )(
        hidden_patch_vectors.reshape(cams, patches, local_width),
        entry_rms_multiplier.reshape(HEADS, 1, DEPTH),
        lookup_projection_matrix.transpose(1, 0, 2),
        exit_projection_matrix,
        probe_sharpness,
        adjacent_camera_pairs.T,
        prior_frame_allowed.T,
    )
    return result.reshape(frames, cams, patches, local_width)


def solution(mesh):
    placed = (
        P("camtime", None, None, "heads"),
        P(),
        P(None, None, "heads"),
        P("heads", None),
        P("heads"),
        P(),
        P(),
    )
    return jax.shard_map(
        on_device,
        mesh=mesh,
        in_specs=placed,
        out_specs=P("camtime", None, None, "heads"),
        check_vma=False,
    )
```

time: 91.3 us -> 72.6 us (0.80)
  Pallas kernels: 84.5 us -> 70.2 us
  local copies, waits for them, and re-layouts: 5.48 us -> 1.62 us
    pallas_call x1, Pallas kernels: 84.5 us -> 70.2 us  [on_device(): pl.pallas_call(kernel, out_shape=jax.ShapeDtypeStruct((cams, patches, loc...]
    reshape x1 -> x0, local copies, waits for them, and re-layouts: 1.95 us -> none  [on_device(): lookup_projection_matrix.reshape(WIDTH, 3 * DEPTH)]
    unnamed x14 -> x1, local copies, waits for them, and re-layouts: 3.53 us -> 1.62 us
where the time goes in v2:
time: 72.6 us; the launch traced here: 72.4 us
  Pallas kernels  70.2 us (97%)
  local copies, waits for them, and re-layouts  1.62 us (2%)
    pallas_call x1, Pallas kernels, on_device(): pl.pallas_call(kernel, out_shape=jax.ShapeDtypeStruct((cams, patches, loc...  70.2 us
    unnamed x1, local copies, waits for them, and re-layouts  1.62 us

profile of v2, /device:TPU:193, one launch (start us, length us, event | category | flops | bytes accessed | tf_op | source)
XLA Modules:
  0.0 72.4 jit_solution(1518906978098535415)
XLA Ops:
  0.7 70.2 %shard_map.73 = bf16[6,128,128]{2,1,0:T(8,128)(2,1)} custom-call(bf16[6,128,128]{2,1,0:T(8,128)(2,1)} %bitcast.8, f32[16,1,128]{2,1,0:T(1,128)} %bitcast.9, bf16[3,2048,128]{2,1,0:T(8,128)(2,1)} %bitcast.6, bf16[128,2048]{1,0:T(8,128)(2,1)} %e_hbm.1, f32[1]{0:T(128)S(6)} %copy.9.sharp_ref, s32[2,6]{1,0:T(2,128)} %bitcast.11, s32[6,16]{1,0:T(8,128)} %bitcast.10), custom_call_target="tpu_custom_call" | custom-call | tf_op jit(solution)/shard_map/pallas_call | solution.py:362
  70.8 1.6 %copy.10 = bf16[1,6,128,128]{3,2,1,0:T(8,128)(2,1)} copy(bf16[1,6,128,128]{3,2,1,0:T(8,128)(2,1)} %bitcast.7) | data formatting | bytes 393216

commit v3 on v2

v3 whole, which is shorter than its diff:
```python
import jax
import jax.numpy as jnp
from jax import lax
from jax.experimental import pallas as pl
from jax.experimental.pallas import tpu as pltpu
from jax.sharding import PartitionSpec as P

HEADS = 16
ROW = 4
PLANES = 8
GROUP = 3
DEPTH = 128
PATCH = 128
WIDTH = HEADS * DEPTH
ROWS = 2 * PATCH
MASKED = -3e38
LOWEST = -1e30
LOG2E = 1.4426950408889634
SINGLE_SEMS = 14
PART = 4 * DEPTH
UP = (3, 4, 4)
DOWN = (4, 3, 3)


def unit_rows(raw):
    return raw * lax.rsqrt(jnp.mean(raw * raw, axis=-1, keepdims=True) + 1e-06)


def kernel(
    x_hbm, gain_hbm, w_hbm, e_hbm, sharp_ref, adj_ref, allowed_ref, out_ref,
    xg, mg, mstage, kv, kc, gain_ref, w_both, e_both, scaled, x_part, x_land, m_part, m_land, m_own,
    raw_ref, qt, top_ref, total_ref, acc_ref,
    x_recv, x_part_recv, m_recv, m_part_recv, up_recv, dn_recv, sems,
):
    (x_send, x_part_send, m_send, m_part_send, up_send, dn_send, c_recv, c_send,
     e_recv, e_send, w_load, w_recv, w_send, gain_sem) = [sems.at[n] for n in range(SINGLE_SEMS)]
    t = lax.axis_index("camtime")
    h = lax.axis_index("heads")
    z, j = t // 2, t % 2
    a, y, p = h // 8, (h // 2) % ROW, h % 2

    def head(a_, y_, p_):
        return a_ * 8 + y_ * 2 + p_

    rows = [y, (y + 1) % ROW, (y + 3) % ROW, (y + 2) % ROW]
    h_sib = head(a, y, 1 - p)
    t_x = z * 2 + 1 - j
    t_up = ((z + 1) % PLANES) * 2 + j
    t_dn = ((z + PLANES - 1) % PLANES) * 2 + j
    mine = GROUP * j
    theirs = GROUP * (1 - j)

    def remote(src, dst, send, recv, heads=None, camtime=None):
        return pltpu.make_async_remote_copy(
            src_ref=src, dst_ref=dst, send_sem=send, recv_sem=recv,
            device_id={"camtime": t if camtime is None else camtime, "heads": h if heads is None else heads},
            device_id_type=pl.DeviceIdType.MESH,
        )

    def arrived(ref, sem):
        pltpu.make_async_copy(ref, ref, sem).wait()

    barrier = pltpu.get_barrier_semaphore()

    def greet(camtime, heads):
        pl.semaphore_signal(
            barrier, inc=1, device_id={"camtime": camtime, "heads": heads}, device_id_type=pl.DeviceIdType.MESH
        )

    for other in range(2, HEADS, 2):
        greet(t, (h + other) % HEADS)
    for other in range(0, HEADS, 2):
        greet(t_x, (h + other) % HEADS)
    greet(t, h_sib)
    greet(t_up, h)
    greet(t_dn, h)

    frame_of = (1 - j, j)

    def x_slot(c, pos, a_, y_):
        return ((c * 2 + pos) * 2 + a_) * ROW + y_

    def m_slot(cam, a_, y_):
        return (cam * 2 + a_) * ROW + y_

    for c in range(GROUP):
        pltpu.make_async_copy(x_hbm.at[mine + c], xg.at[x_slot(c, 1, a, y)], x_recv.at[c, 1]).start()
    gain_load = pltpu.make_async_copy(gain_hbm.at[:, p], gain_ref, gain_sem)
    gain_load.start()
    for i in range(3):
        pltpu.make_async_copy(w_hbm.at[i, :, p], w_both.at[:, :, i * DEPTH:(i + 1) * DEPTH], w_load).start()
    for c in range(GROUP):
        top_ref[c] = jnp.full((1, ROWS), LOWEST, jnp.float32)
        total_ref[c] = jnp.zeros((1, ROWS), jnp.float32)
        acc_ref[c] = jnp.zeros((DEPTH, ROWS), jnp.float32)
    pl.semaphore_wait(barrier, HEADS + 2)

    chips = [(a_, y_) for y_ in rows for a_ in (1 - a, a)]

    def x_push(c):
        for a_, y_ in chips:
            remote(x_hbm.at[theirs + c], xg.at[x_slot(c, 0, a, y)], x_send, x_recv.at[c, 0],
                   heads=head(a_, y_, p), camtime=t_x).start()
        for n, (a_, y_) in enumerate(chips):
            if n != 1:
                remote(x_hbm.at[mine + c], xg.at[x_slot(c, 1, a, y)], x_send, x_recv.at[c, 1],
                       heads=head(a_, y_, p)).start()

    def w_copy(i):
        return remote(
            w_hbm.at[i, :, 1 - p], w_both.at[:, :, (3 + i) * DEPTH:(4 + i) * DEPTH], w_send, w_recv, heads=h_sib
        )

    def e_push():
        for n, (a_, y_) in enumerate(chips):
            for side, p_ in enumerate((p, 1 - p)):
                src = e_hbm.at[:, pl.ds(pl.multiple_of(head(a_, y_, p_) * DEPTH, DEPTH), DEPTH)]
                dst = e_both.at[a * ROW + y, :, side * DEPTH:(side + 1) * DEPTH]
                if n == 1:
                    pltpu.make_async_copy(src, dst, e_recv).start()
                else:
                    remote(src, dst, e_send, e_recv, heads=head(a_, y_, p)).start()

    scale = sharp_ref[0] * (LOG2E / DEPTH**0.5)

    def up_copy(c, pos, d):
        src = kc.at[mine + c, frame_of[pos]] if d == 0 else kv.at[z - d, c, pos]
        return remote(src, kv.at[z - d, c, pos], up_send, up_recv.at[c, pos, d], camtime=t_up)

    def dn_copy(c, pos, hop):
        plane = (z + hop) % PLANES
        src = kc.at[mine + c, frame_of[pos]] if hop == 0 else kv.at[plane, c, pos]
        return remote(src, kv.at[plane, c, pos], dn_send, dn_recv.at[c, pos, hop], camtime=t_dn)

    def cross_copy(c):
        return remote(kc.at[mine + c], kc.at[mine + c], c_send, c_recv, camtime=t_x)

    def part_copy(c, places):
        lo, count = places[0], len(places)
        return remote(
            x_part.at[c, pl.ds(lo, count)], x_land.at[c, pl.ds(lo, count)],
            x_part_send, x_part_recv.at[c, lo], heads=h_sib,
        )

    def project_half(c, places):
        count = len(places) * PATCH
        squares = jnp.zeros((count, DEPTH), jnp.float32)
        for pos in places:
            arrived(xg.at[pl.ds(x_slot(c, pos, 0, 0), HEADS // 2)], x_recv.at[c, pos])
        for n in range(HEADS // 2):
            wide = jnp.concatenate([xg[x_slot(c, pos, 0, n)] for pos in places], axis=0).astype(jnp.float32)
            squares = squares + wide * wide
            scaled[:count, n * DEPTH:(n + 1) * DEPTH] = (wide * gain_ref[n]).astype(jnp.bfloat16)
        part = jnp.dot(
            scaled[:count], w_both[...].reshape(WIDTH // 2, 6 * DEPTH), preferred_element_type=jnp.float32
        )
        for n, pos in enumerate(places):
            here = slice(n * PATCH, (n + 1) * PATCH)
            x_part[c, pos, :, :3 * DEPTH] = part[here, 3 * DEPTH:]
            x_part[c, pos, :, 3 * DEPTH:] = squares[here]
            raw_ref[c, pos] = part[here, :3 * DEPTH]
        part_copy(c, places).start()

    def project(c, places):
        lo, count = places[0], len(places)
        arrived(x_land.at[c, pl.ds(lo, count)], x_part_recv.at[c, lo])
        land = x_land[c, lo:lo + count].reshape(count * PATCH, PART)
        squares = x_part[c, lo:lo + count].reshape(count * PATCH, PART)[:, 3 * DEPTH:] + land[:, 3 * DEPTH:]
        inv_rms = lax.rsqrt(jnp.sum(squares, axis=1, keepdims=True) / WIDTH + 1e-06)
        raw = (raw_ref[c, lo:lo + count].reshape(count * PATCH, 3 * DEPTH) + land[:, :3 * DEPTH]) * inv_rms
        key = unit_rows(raw[:, DEPTH:2 * DEPTH]).astype(jnp.bfloat16)
        value = raw[:, 2 * DEPTH:]
        for n, pos in enumerate(places):
            kc[mine + c, frame_of[pos], 0] = key[n * PATCH:(n + 1) * PATCH]
            kc[mine + c, frame_of[pos], 1] = value[n * PATCH:(n + 1) * PATCH].T.astype(jnp.bfloat16)

            @pl.when(z < PLANES - 1)
            def _():
                up_copy(c, pos, 0).start()

            @pl.when(z < DOWN[c])
            def _():
                dn_copy(c, pos, 0).start()

        if 1 in places:
            cross_copy(c).start()
        query = unit_rows(raw[:, :DEPTH])
        for n, pos in enumerate(places):
            qt[c, :, pos * PATCH:(pos + 1) * PATCH] = query[n * PATCH:(n + 1) * PATCH].T.astype(jnp.bfloat16)

    def bias(plane, f, c, later=True):
        return jnp.where((allowed_ref[mine + c, 2 * plane + f] == 1) & later, 0.0, MASKED).astype(jnp.float32)

    def fold(c, score, values, lanes):
        before = top_ref[c, :, lanes]
        top = jnp.maximum(before, jnp.max(score, axis=0, keepdims=True))
        expo = jnp.exp2(score - top)
        rescale = jnp.exp2(before - top)
        top_ref[c, :, lanes] = top
        total_ref[c, :, lanes] = total_ref[c, :, lanes] * rescale + jnp.sum(expo, axis=0, keepdims=True)
        acc_ref[c, :, lanes] = acc_ref[c, :, lanes] * rescale + jnp.dot(
            values, expo.astype(jnp.bfloat16), preferred_element_type=jnp.float32
        )

    def attend(c, plane):
        keys = jnp.concatenate([kv[plane, c, 0, 0], kv[plane, c, 1, 0]], axis=0)
        values = jnp.concatenate([kv[plane, c, 0, 1], kv[plane, c, 1, 1]], axis=1)
        score = jnp.dot(keys, qt[c], preferred_element_type=jnp.float32) * scale
        score = jnp.concatenate(
            [score[:PATCH] + bias(plane, frame_of[0], c), score[PATCH:] + bias(plane, frame_of[1], c)], axis=0
        )
        fold(c, score, values, slice(0, ROWS))

    def attend_cross(c):
        if c == 0:
            arrived(kc.at[pl.ds(theirs, GROUP)], c_recv)
        cam = mine + c
        for pos, f in enumerate(frame_of):
            lanes = slice(pos * PATCH, (pos + 1) * PATCH)
            near = [(cam, f), (adj_ref[0, cam], f), (adj_ref[1, cam], f), (cam, 0)]
            keys = jnp.concatenate([kc[n, f_, 0] for n, f_ in near], axis=0)
            values = jnp.concatenate([kc[n, f_, 1] for n, f_ in near], axis=1)
            score = jnp.dot(keys, qt[c, :, lanes], preferred_element_type=jnp.float32) * scale
            score = jnp.concatenate(
                [score[:3 * PATCH], score[3 * PATCH:] + bias(z, 0, c, f == 1)], axis=0
            )
            fold(c, score, values, lanes)

    def step_up(c, d):
        @pl.when(z >= d)
        def _():
            for pos in range(2):
                arrived(kv.at[z - d, c, pos], up_recv.at[c, pos, d - 1])
                if d < UP[c]:
                    @pl.when(z < PLANES - 1)
                    def _():
                        up_copy(c, pos, d).start()
            attend(c, z - d)

    def step_dn(c, hop):
        plane = (z + hop) % PLANES

        @pl.when(plane < DOWN[c])
        def _():
            for pos in range(2):
                arrived(kv.at[plane, c, pos], dn_recv.at[c, pos, hop - 1])
                if hop < DOWN[c]:
                    dn_copy(c, pos, hop).start()

            @pl.when(plane < z)
            def _():
                attend(c, plane)

    def m_push(c):
        mixed = (acc_ref[c] / total_ref[c]).T.astype(jnp.bfloat16).reshape(2, PATCH, DEPTH)
        mstage[c] = mixed
        cam = mine + c
        slot = m_slot(cam, a, y)
        for a_, y_ in chips:
            remote(mstage.at[c, 0], mg.at[slot], m_send, m_recv.at[c], heads=head(a_, y_, p), camtime=t_x).start()
        for n, (a_, y_) in enumerate(chips):
            if n != 1:
                remote(mstage.at[c, 1], mg.at[slot], m_send, m_recv.at[c], heads=head(a_, y_, p)).start()
        mg[slot] = mstage[c, 1]

    def m_copy(c):
        return remote(m_part.at[c], m_land.at[c], m_part_send, m_part_recv.at[c], heads=h_sib)

    def project_out_half(c):
        arrived(xg.at[pl.ds(0, HEADS - 1)], m_recv.at[c])
        summed = jnp.zeros((ROWS, 2 * DEPTH), jnp.float32)
        for n in range(HEADS // 2):
            mixed = jnp.concatenate([mg[m_slot(cam, 0, n)] for cam in (mine + c, theirs + c)], axis=0)
            part = jnp.dot(mixed, e_both[n], preferred_element_type=jnp.float32)
            summed = summed + part.astype(jnp.bfloat16).astype(jnp.float32)
        m_part[c] = summed[:, DEPTH:]
        m_copy(c).start()
        m_own[c] = summed[:, :DEPTH]

    def project_out(c):
        arrived(m_land.at[c], m_part_recv.at[c])
        summed = (m_own[c] + m_land[c]).astype(jnp.bfloat16)
        out_ref[mine + c] = summed[:PATCH]
        out_ref[theirs + c] = summed[PATCH:]

    x_push(0)
    for i in range(3):
        w_copy(i).start()
    x_push(1)
    x_push(2)
    gain_load.wait()
    arrived(w_both.at[:, :, :3 * DEPTH], w_load)
    arrived(w_both.at[:, :, 3 * DEPTH:], w_recv)
    project_half(0, (0,))
    project(0, (0,))
    project_half(0, (1,))
    project(0, (1,))
    project_half(1, (0,))
    step_up(0, 1)
    step_dn(0, 1)
    project_half(1, (1,))
    project(1, (0,))
    project(1, (1,))
    project_half(2, (0,))
    step_up(0, 2)
    project(2, (0,))
    project_half(2, (1,))
    step_dn(0, 2)
    step_up(1, 1)
    project(2, (1,))
    e_push()
    step_dn(1, 1)
    step_dn(0, 3)
    step_up(1, 2)
    step_dn(1, 2)
    step_up(2, 1)
    step_dn(2, 1)
    attend_cross(0)
    step_up(0, 3)
    step_dn(0, 4)
    m_push(0)
    attend_cross(1)
    step_up(1, 3)
    step_up(2, 2)
    step_dn(1, 3)
    attend_cross(2)
    step_up(1, 4)
    step_dn(2, 2)
    m_push(1)
    step_up(2, 3)
    step_dn(2, 3)
    step_up(2, 4)
    m_push(2)
    arrived(e_both, e_recv)
    project_out_half(0)
    project_out_half(1)
    project_out(0)
    project_out(1)
    project_out_half(2)
    project_out(2)

    pieces = HEADS - 1
    arrived(xg.at[pl.ds(0, GROUP * pieces)], x_send)
    arrived(xg.at[pl.ds(0, GROUP * pieces)], m_send)
    arrived(xg.at[pl.ds(0, HEADS - 2)], e_send)
    arrived(xg.at[pl.ds(0, 3 * HEADS // 2)], w_send)
    arrived(x_part, x_part_send)
    arrived(m_part, m_part_send)
    arrived(kc.at[pl.ds(mine, GROUP)], c_send)
    for plane in range(PLANES):
        ups = sum(min(UP[c], plane + 1) for c in range(GROUP)) if plane < PLANES - 1 else 0
        downs = sum((plane + hop) % PLANES < DOWN[c] for c in range(GROUP) for hop in range(DOWN[c]))

        @pl.when(z == plane)
        def _():
            if ups:
                arrived(xg.at[pl.ds(0, 4 * ups)], up_send)
            if downs:
                arrived(xg.at[pl.ds(0, 4 * downs)], dn_send)


def on_device(
    hidden_patch_vectors,
    entry_rms_multiplier,
    lookup_projection_matrix,
    exit_projection_matrix,
    probe_sharpness,
    adjacent_camera_pairs,
    prior_frame_allowed,
):
    frames, cams, patches, local_width = hidden_patch_vectors.shape
    vmem = pl.BlockSpec(memory_space=pltpu.VMEM)
    smem = pl.BlockSpec(memory_space=pltpu.SMEM)
    hbm = pl.BlockSpec(memory_space=pltpu.HBM)
    dma = pltpu.SemaphoreType.DMA
    bf16, f32 = jnp.bfloat16, jnp.float32
    result = pl.pallas_call(
        kernel,
        out_shape=jax.ShapeDtypeStruct((cams, patches, local_width), bf16),
        in_specs=[hbm, hbm, hbm, hbm, smem, smem, smem],
        out_specs=vmem,
        scratch_shapes=[
            pltpu.VMEM((GROUP * HEADS, PATCH, DEPTH), bf16),
            pltpu.VMEM((GROUP * HEADS, PATCH, DEPTH), bf16),
            pltpu.VMEM((GROUP, 2, PATCH, DEPTH), bf16),
            pltpu.VMEM((PLANES, GROUP, 2, 2, PATCH, DEPTH), bf16),
            pltpu.VMEM((2 * GROUP, 2, 2, PATCH, DEPTH), bf16),
            pltpu.VMEM((HEADS // 2, 1, DEPTH), f32),
            pltpu.VMEM((HEADS // 2, DEPTH, 6 * DEPTH), bf16),
            pltpu.VMEM((HEADS // 2, DEPTH, 2 * DEPTH), bf16),
            pltpu.VMEM((ROWS, WIDTH // 2), bf16),
            pltpu.VMEM((GROUP, 2, PATCH, PART), f32),
            pltpu.VMEM((GROUP, 2, PATCH, PART), f32),
            pltpu.VMEM((GROUP, ROWS, DEPTH), f32),
            pltpu.VMEM((GROUP, ROWS, DEPTH), f32),
            pltpu.VMEM((GROUP, ROWS, DEPTH), f32),
            pltpu.VMEM((GROUP, 2, PATCH, 3 * DEPTH), f32),
            pltpu.VMEM((GROUP, DEPTH, ROWS), bf16),
            pltpu.VMEM((GROUP, 1, ROWS), f32),
            pltpu.VMEM((GROUP, 1, ROWS), f32),
            pltpu.VMEM((GROUP, DEPTH, ROWS), f32),
            dma((GROUP, 2)),
            dma((GROUP, 2)),
            dma((GROUP,)),
            dma((GROUP,)),
            dma((GROUP, 2, 4)),
            dma((GROUP, 2, 4)),
            dma((SINGLE_SEMS,)),
        ],
        compiler_params=pltpu.CompilerParams(
            collective_id=0, has_side_effects=True, vmem_limit_bytes=60 * 1024 * 1024
        ),
    )(
        hidden_patch_vectors.reshape(cams, patches, local_width),
        entry_rms_multiplier.reshape(HEADS // 2, 2, 1, DEPTH),
        lookup_projection_matrix.transpose(1, 0, 2).reshape(3, HEADS // 2, 2, DEPTH, DEPTH),
        exit_projection_matrix,
        probe_sharpness,
        adjacent_camera_pairs.T,
        prior_frame_allowed.T,
    )
    return result.reshape(frames, cams, patches, local_width)


def solution(mesh):
    placed = (
        P("camtime", None, None, "heads"),
        P(),
        P(None, None, "heads"),
        P("heads", None),
        P("heads"),
        P(),
        P(),
    )
    return jax.shard_map(
        on_device,
        mesh=mesh,
        in_specs=placed,
        out_specs=P("camtime", None, None, "heads"),
        check_vma=False,
    )
```

time: 72.6 us -> 69.3 us (0.955)
  Pallas kernels: 70.2 us -> 66.9 us
    pallas_call x1, Pallas kernels: 70.2 us -> 66.9 us  [on_device(): pl.pallas_call(kernel, out_shape=jax.ShapeDtypeStruct((cams, patches, loc...]
where the time goes in v3:
time: 69.3 us; the launch traced here: 69.2 us
  Pallas kernels  66.9 us (97%)
  local copies, waits for them, and re-layouts  1.62 us (2%)
    pallas_call x1, Pallas kernels, on_device(): pl.pallas_call(kernel, out_shape=jax.ShapeDtypeStruct((cams, patches, loc...  66.9 us
    unnamed x1, local copies, waits for them, and re-layouts  1.62 us

profile of v3, /device:TPU:193, one launch (start us, length us, event | category | flops | bytes accessed | tf_op | source)
XLA Modules:
  0.0 69.2 jit_solution(4324560389821415969)
XLA Ops:
  0.7 66.9 %shard_map.73 = bf16[6,128,128]{2,1,0:T(8,128)(2,1)} custom-call(bf16[6,128,128]{2,1,0:T(8,128)(2,1)} %bitcast.10, f32[8,2,1,128]{3,2,1,0:T(1,128)} %bitcast.11, bf16[3,8,2,128,128]{4,3,2,1,0:T(8,128)(2,1)} %bitcast.8, bf16[128,2048]{1,0:T(8,128)(2,1)} %e_hbm.1, f32[1]{0:T(128)S(6)} %copy.9.sharp_ref, s32[2,6]{1,0:T(2,128)} %bitcast.13, s32[6,16]{1,0:T(8,128)} %bitcast.12), custom_call_target="tpu_custom_call" | custom-call | tf_op jit(solution)/shard_map/pallas_call | solution.py:377
  67.6 1.6 %copy.10 = bf16[1,6,128,128]{3,2,1,0:T(8,128)(2,1)} copy(bf16[1,6,128,128]{3,2,1,0:T(8,128)(2,1)} %bitcast.9) | data formatting | bytes 393216

commit v4 on v3

--- a/solution.py
+++ b/solution.py
@@ -16,10 +16,20 @@
 MASKED = -3e38
 LOWEST = -1e30
 LOG2E = 1.4426950408889634
-SINGLE_SEMS = 14
+SINGLE_SEMS = 18
 PART = 4 * DEPTH
-UP = (3, 4, 4)
-DOWN = (4, 3, 3)
+UP = ((3, 4), (3, 3), (4, 4))
+DOWN = ((4, 3), (4, 4), (3, 3))
+TREE_X = (2,)
+ORDER = (
+    "H00", "P00", "X20", "H01", "P01", "X21", "H10", "U001", "D001", "P10", "H11", "U011",
+    "D011", "P11", "H20", "U101", "U002", "D002", "D101", "U012", "P20", "H21",
+    "D012", "U003", "D111", "D003", "P21", "E", "D102", "U013", "D013", "C0",
+    "U111", "C2", "U201", "C1", "D112", "D201", "D004", "U102", "U014", "F0",
+    "U211", "U112", "D103", "D113", "D211", "U202", "U103", "D104", "U212", "D202",
+    "U113", "D114", "F1", "U203", "D212", "U213", "D203", "U204", "D213", "U214",
+    "F2",
+)
 
 
 def unit_rows(raw):
@@ -27,13 +37,13 @@
 
 
 def kernel(
-    x_hbm, gain_hbm, w_hbm, e_hbm, sharp_ref, adj_ref, allowed_ref, out_ref,
+    x_hbm, gain_hbm, w_hbm, e_hbm, sharp_hbm, adj_hbm, allowed_hbm, out_hbm,
     xg, mg, mstage, kv, kc, gain_ref, w_both, e_both, scaled, x_part, x_land, m_part, m_land, m_own,
-    raw_ref, qt, top_ref, total_ref, acc_ref,
-    x_recv, x_part_recv, m_recv, m_part_recv, up_recv, dn_recv, sems,
+    raw_ref, qt, top_ref, total_ref, acc_ref, out_ref, sharp_ref, adj_ref, allowed_ref,
+    x_recv, x_row, x_part_recv, m_recv, m_part_recv, up_recv, dn_recv, sems,
 ):
     (x_send, x_part_send, m_send, m_part_send, up_send, dn_send, c_recv, c_send,
-     e_recv, e_send, w_load, w_recv, w_send, gain_sem) = [sems.at[n] for n in range(SINGLE_SEMS)]
+     e_recv, e_send, w_load, w_recv, w_send, gain_sem, sharp_sem, adj_sem, allowed_sem, out_sem) = [sems.at[n] for n in range(SINGLE_SEMS)]
     t = lax.axis_index("camtime")
     h = lax.axis_index("heads")
     z, j = t // 2, t % 2
@@ -78,15 +88,22 @@
     frame_of = (1 - j, j)
 
     def x_slot(c, pos, a_, y_):
-        return ((c * 2 + pos) * 2 + a_) * ROW + y_
+        return ((c * 2 + pos) * ROW + y_) * 2 + a_
 
     def m_slot(cam, a_, y_):
-        return (cam * 2 + a_) * ROW + y_
+        return (cam * ROW + y_) * 2 + a_
 
     for c in range(GROUP):
-        pltpu.make_async_copy(x_hbm.at[mine + c], xg.at[x_slot(c, 1, a, y)], x_recv.at[c, 1]).start()
+        pltpu.make_async_copy(x_hbm.at[mine + c], xg.at[x_slot(c, 1, a, y)], (x_row if c in TREE_X else x_recv).at[c, 1]).start()
     gain_load = pltpu.make_async_copy(gain_hbm.at[:, p], gain_ref, gain_sem)
     gain_load.start()
+    small_loads = [
+        pltpu.make_async_copy(sharp_hbm, sharp_ref, sharp_sem),
+        pltpu.make_async_copy(adj_hbm, adj_ref, adj_sem),
+        pltpu.make_async_copy(allowed_hbm, allowed_ref, allowed_sem),
+    ]
+    for load in small_loads:
+        load.start()
     for i in range(3):
         pltpu.make_async_copy(w_hbm.at[i, :, p], w_both.at[:, :, i * DEPTH:(i + 1) * DEPTH], w_load).start()
     for c in range(GROUP):
@@ -97,7 +114,18 @@
 
     chips = [(a_, y_) for y_ in rows for a_ in (1 - a, a)]
 
+    def row_push(buf, slot, send, recv):
+        for y_ in rows[1:]:
+            remote(buf.at[pl.ds(slot, 2)], buf.at[pl.ds(slot, 2)], send, recv, heads=head(a, y_, p)).start()
+
     def x_push(c):
+        if c in TREE_X:
+            for a_ in (1 - a, a):
+                remote(x_hbm.at[theirs + c], xg.at[x_slot(c, 0, a, y)], x_send, x_row.at[c, 0],
+                       heads=head(a_, y, p), camtime=t_x).start()
+            remote(x_hbm.at[mine + c], xg.at[x_slot(c, 1, a, y)], x_send, x_row.at[c, 1],
+                   heads=head(1 - a, y, p)).start()
+            return
         for a_, y_ in chips:
             remote(x_hbm.at[theirs + c], xg.at[x_slot(c, 0, a, y)], x_send, x_recv.at[c, 0],
                    heads=head(a_, y_, p), camtime=t_x).start()
@@ -105,6 +133,11 @@
             if n != 1:
                 remote(x_hbm.at[mine + c], xg.at[x_slot(c, 1, a, y)], x_send, x_recv.at[c, 1],
                        heads=head(a_, y_, p)).start()
+
+    def x_relay(c, pos):
+        slot = x_slot(c, pos, 0, y)
+        arrived(xg.at[pl.ds(slot, 2)], x_row.at[c, pos])
+        row_push(xg, slot, x_send, x_recv.at[c, pos])
 
     def w_copy(i):
         return remote(
@@ -121,7 +154,6 @@
                 else:
                     remote(src, dst, e_send, e_recv, heads=head(a_, y_, p)).start()
 
-    scale = sharp_ref[0] * (LOG2E / DEPTH**0.5)
 
     def up_copy(c, pos, d):
         src = kc.at[mine + c, frame_of[pos]] if d == 0 else kv.at[z - d, c, pos]
@@ -146,9 +178,9 @@
         count = len(places) * PATCH
         squares = jnp.zeros((count, DEPTH), jnp.float32)
         for pos in places:
-            arrived(xg.at[pl.ds(x_slot(c, pos, 0, 0), HEADS // 2)], x_recv.at[c, pos])
+            arrived(xg.at[pl.ds(x_slot(c, pos, 0, 0), 6 if c in TREE_X else 8)], x_recv.at[c, pos])
         for n in range(HEADS // 2):
-            wide = jnp.concatenate([xg[x_slot(c, pos, 0, n)] for pos in places], axis=0).astype(jnp.float32)
+            wide = jnp.concatenate([xg[x_slot(c, pos, n // ROW, n % ROW)] for pos in places], axis=0).astype(jnp.float32)
             squares = squares + wide * wide
             scaled[:count, n * DEPTH:(n + 1) * DEPTH] = (wide * gain_ref[n]).astype(jnp.bfloat16)
         part = jnp.dot(
@@ -178,7 +210,7 @@
             def _():
                 up_copy(c, pos, 0).start()
 
-            @pl.when(z < DOWN[c])
+            @pl.when(z < DOWN[c][pos])
             def _():
                 dn_copy(c, pos, 0).start()
 
@@ -205,14 +237,17 @@
     def attend(c, plane):
         keys = jnp.concatenate([kv[plane, c, 0, 0], kv[plane, c, 1, 0]], axis=0)
         values = jnp.concatenate([kv[plane, c, 0, 1], kv[plane, c, 1, 1]], axis=1)
-        score = jnp.dot(keys, qt[c], preferred_element_type=jnp.float32) * scale
+        score = jnp.dot(keys, qt[c], preferred_element_type=jnp.float32) * (sharp_ref[0, 0] * (LOG2E / DEPTH**0.5))
         score = jnp.concatenate(
             [score[:PATCH] + bias(plane, frame_of[0], c), score[PATCH:] + bias(plane, frame_of[1], c)], axis=0
         )
         fold(c, score, values, slice(0, ROWS))
 
+    crossed = []
+
     def attend_cross(c):
-        if c == 0:
+        if not crossed:
+            crossed.append(c)
             arrived(kc.at[pl.ds(theirs, GROUP)], c_recv)
         cam = mine + c
         for pos, f in enumerate(frame_of):
@@ -220,48 +255,53 @@
             near = [(cam, f), (adj_ref[0, cam], f), (adj_ref[1, cam], f), (cam, 0)]
             keys = jnp.concatenate([kc[n, f_, 0] for n, f_ in near], axis=0)
             values = jnp.concatenate([kc[n, f_, 1] for n, f_ in near], axis=1)
-            score = jnp.dot(keys, qt[c, :, lanes], preferred_element_type=jnp.float32) * scale
+            score = jnp.dot(keys, qt[c, :, lanes], preferred_element_type=jnp.float32) * (sharp_ref[0, 0] * (LOG2E / DEPTH**0.5))
             score = jnp.concatenate(
                 [score[:3 * PATCH], score[3 * PATCH:] + bias(z, 0, c, f == 1)], axis=0
             )
             fold(c, score, values, lanes)
 
-    def step_up(c, d):
+    deliveries = {}
+    for n, step in enumerate(ORDER):
+        if step[0] in "UD":
+            below = int(step[3]) if step[0] == "U" else PLANES - int(step[3])
+            deliveries[step[1], below] = n
+
+    def step_up(n, c, pos, d):
         @pl.when(z >= d)
         def _():
-            for pos in range(2):
-                arrived(kv.at[z - d, c, pos], up_recv.at[c, pos, d - 1])
-                if d < UP[c]:
-                    @pl.when(z < PLANES - 1)
-                    def _():
-                        up_copy(c, pos, d).start()
-            attend(c, z - d)
-
-    def step_dn(c, hop):
+            arrived(kv.at[z - d, c, pos], up_recv.at[c, pos, d - 1])
+            if d < UP[c][pos]:
+                @pl.when(z < PLANES - 1)
+                def _():
+                    up_copy(c, pos, d).start()
+            if deliveries[str(c), d] == n:
+                attend(c, z - d)
+
+    def step_dn(n, c, pos, hop):
         plane = (z + hop) % PLANES
 
-        @pl.when(plane < DOWN[c])
+        @pl.when(plane < DOWN[c][pos])
         def _():
-            for pos in range(2):
-                arrived(kv.at[plane, c, pos], dn_recv.at[c, pos, hop - 1])
-                if hop < DOWN[c]:
-                    dn_copy(c, pos, hop).start()
-
-            @pl.when(plane < z)
-            def _():
-                attend(c, plane)
+            arrived(kv.at[plane, c, pos], dn_recv.at[c, pos, hop - 1])
+            if hop < DOWN[c][pos]:
+                dn_copy(c, pos, hop).start()
+            if deliveries[str(c), PLANES - hop] == n:
+                @pl.when(plane < z)
+                def _():
+                    attend(c, plane)
 
     def m_push(c):
         mixed = (acc_ref[c] / total_ref[c]).T.astype(jnp.bfloat16).reshape(2, PATCH, DEPTH)
         mstage[c] = mixed
         cam = mine + c
         slot = m_slot(cam, a, y)
+        mg[slot] = mstage[c, 1]
         for a_, y_ in chips:
             remote(mstage.at[c, 0], mg.at[slot], m_send, m_recv.at[c], heads=head(a_, y_, p), camtime=t_x).start()
         for n, (a_, y_) in enumerate(chips):
             if n != 1:
                 remote(mstage.at[c, 1], mg.at[slot], m_send, m_recv.at[c], heads=head(a_, y_, p)).start()
-        mg[slot] = mstage[c, 1]
 
     def m_copy(c):
         return remote(m_part.at[c], m_land.at[c], m_part_send, m_part_recv.at[c], heads=h_sib)
@@ -270,7 +310,7 @@
         arrived(xg.at[pl.ds(0, HEADS - 1)], m_recv.at[c])
         summed = jnp.zeros((ROWS, 2 * DEPTH), jnp.float32)
         for n in range(HEADS // 2):
-            mixed = jnp.concatenate([mg[m_slot(cam, 0, n)] for cam in (mine + c, theirs + c)], axis=0)
+            mixed = jnp.concatenate([mg[m_slot(cam, n // ROW, n % ROW)] for cam in (mine + c, theirs + c)], axis=0)
             part = jnp.dot(mixed, e_both[n], preferred_element_type=jnp.float32)
             summed = summed + part.astype(jnp.bfloat16).astype(jnp.float32)
         m_part[c] = summed[:, DEPTH:]
@@ -282,55 +322,41 @@
         summed = (m_own[c] + m_land[c]).astype(jnp.bfloat16)
         out_ref[mine + c] = summed[:PATCH]
         out_ref[theirs + c] = summed[PATCH:]
+        for cam in (mine + c, theirs + c):
+            pltpu.make_async_copy(out_ref.at[cam], out_hbm.at[cam], out_sem).start()
 
     x_push(0)
     for i in range(3):
         w_copy(i).start()
-    x_push(1)
-    x_push(2)
-    gain_load.wait()
+    for c in TREE_X:
+        x_push(c)
+    for c in range(1, GROUP):
+        if c not in TREE_X:
+            x_push(c)
+    for load in [gain_load] + small_loads:
+        load.wait()
     arrived(w_both.at[:, :, :3 * DEPTH], w_load)
     arrived(w_both.at[:, :, 3 * DEPTH:], w_recv)
-    project_half(0, (0,))
-    project(0, (0,))
-    project_half(0, (1,))
-    project(0, (1,))
-    project_half(1, (0,))
-    step_up(0, 1)
-    step_dn(0, 1)
-    project_half(1, (1,))
-    project(1, (0,))
-    project(1, (1,))
-    project_half(2, (0,))
-    step_up(0, 2)
-    project(2, (0,))
-    project_half(2, (1,))
-    step_dn(0, 2)
-    step_up(1, 1)
-    project(2, (1,))
-    e_push()
-    step_dn(1, 1)
-    step_dn(0, 3)
-    step_up(1, 2)
-    step_dn(1, 2)
-    step_up(2, 1)
-    step_dn(2, 1)
-    attend_cross(0)
-    step_up(0, 3)
-    step_dn(0, 4)
-    m_push(0)
-    attend_cross(1)
-    step_up(1, 3)
-    step_up(2, 2)
-    step_dn(1, 3)
-    attend_cross(2)
-    step_up(1, 4)
-    step_dn(2, 2)
-    m_push(1)
-    step_up(2, 3)
-    step_dn(2, 3)
-    step_up(2, 4)
-    m_push(2)
+    for n, step in enumerate(ORDER):
+        kind, c = step[0], int(step[1:2] or 0)
+        pos, hop = int(step[2:3] or 0), int(step[3:] or 0)
+        if kind == "H":
+            project_half(c, (pos,))
+        elif kind == "P":
+            project(c, (pos,))
+        elif kind == "U":
+            step_up(n, c, pos, hop)
+        elif kind == "D":
+            step_dn(n, c, pos, hop)
+        elif kind == "C":
+            attend_cross(c)
+        elif kind == "F":
+            m_push(c)
+        elif kind == "X":
+            if c in TREE_X:
+                x_relay(c, pos)
+        else:
+            e_push()
     arrived(e_both, e_recv)
     project_out_half(0)
     project_out_half(1)
@@ -339,6 +365,7 @@
     project_out_half(2)
     project_out(2)
 
+    arrived(out_ref, out_sem)
     pieces = HEADS - 1
     arrived(xg.at[pl.ds(0, GROUP * pieces)], x_send)
     arrived(xg.at[pl.ds(0, GROUP * pieces)], m_send)
@@ -348,15 +375,16 @@
     arrived(m_part, m_part_send)
     arrived(kc.at[pl.ds(mine, GROUP)], c_send)
     for plane in range(PLANES):
-        ups = sum(min(UP[c], plane + 1) for c in range(GROUP)) if plane < PLANES - 1 else 0
-        downs = sum((plane + hop) % PLANES < DOWN[c] for c in range(GROUP) for hop in range(DOWN[c]))
+        frames = [(c, pos) for c in range(GROUP) for pos in range(2)]
+        ups = sum(min(UP[c][pos], plane + 1) for c, pos in frames) if plane < PLANES - 1 else 0
+        downs = sum((plane + hop) % PLANES < DOWN[c][pos] for c, pos in frames for hop in range(DOWN[c][pos]))
 
         @pl.when(z == plane)
         def _():
             if ups:
-                arrived(xg.at[pl.ds(0, 4 * ups)], up_send)
+                arrived(xg.at[pl.ds(0, 2 * ups)], up_send)
             if downs:
-                arrived(xg.at[pl.ds(0, 4 * downs)], dn_send)
+                arrived(xg.at[pl.ds(0, 2 * downs)], dn_send)
 
 
 def on_device(
@@ -369,16 +397,14 @@
     prior_frame_allowed,
 ):
     frames, cams, patches, local_width = hidden_patch_vectors.shape
-    vmem = pl.BlockSpec(memory_space=pltpu.VMEM)
-    smem = pl.BlockSpec(memory_space=pltpu.SMEM)
     hbm = pl.BlockSpec(memory_space=pltpu.HBM)
     dma = pltpu.SemaphoreType.DMA
     bf16, f32 = jnp.bfloat16, jnp.float32
     result = pl.pallas_call(
         kernel,
         out_shape=jax.ShapeDtypeStruct((cams, patches, local_width), bf16),
-        in_specs=[hbm, hbm, hbm, hbm, smem, smem, smem],
-        out_specs=vmem,
+        in_specs=[hbm] * 7,
+        out_specs=pl.BlockSpec(memory_space=pltpu.VMEM),
         scratch_shapes=[
             pltpu.VMEM((GROUP * HEADS, PATCH, DEPTH), bf16),
             pltpu.VMEM((GROUP * HEADS, PATCH, DEPTH), bf16),
@@ -399,6 +425,11 @@
             pltpu.VMEM((GROUP, 1, ROWS), f32),
             pltpu.VMEM((GROUP, 1, ROWS), f32),
             pltpu.VMEM((GROUP, DEPTH, ROWS), f32),
+            pltpu.VMEM((cams, patches, local_width), bf16),
+            pltpu.SMEM((1, 1), f32),
+            pltpu.SMEM((2, cams), jnp.int32),
+            pltpu.SMEM((cams, PLANES * 2), jnp.int32),
+            dma((GROUP, 2)),
             dma((GROUP, 2)),
             dma((GROUP, 2)),
             dma((GROUP,)),
@@ -408,17 +439,17 @@
             dma((SINGLE_SEMS,)),
         ],
         compiler_params=pltpu.CompilerParams(
-            collective_id=0, has_side_effects=True, vmem_limit_bytes=60 * 1024 * 1024
+            collective_id=0, has_side_effects=True, vmem_limit_bytes=48 * 1024 * 1024
         ),
-    )(
+    )(*[operand if operand.size == 1 else pltpu.with_memory_space_constraint(operand, pltpu.HBM) for operand in (
         hidden_patch_vectors.reshape(cams, patches, local_width),
         entry_rms_multiplier.reshape(HEADS // 2, 2, 1, DEPTH),
         lookup_projection_matrix.transpose(1, 0, 2).reshape(3, HEADS // 2, 2, DEPTH, DEPTH),
         exit_projection_matrix,
-        probe_sharpness,
+        probe_sharpness.reshape(1, 1),
         adjacent_camera_pairs.T,
         prior_frame_allowed.T,
-    )
+    )])
     return result.reshape(frames, cams, patches, local_width)
 
 

time: 69.3 us -> 66.2 us (0.955)
  Pallas kernels: 66.9 us -> 64.7 us
  local copies, waits for them, and re-layouts: 1.62 us -> 0.68 us
    pallas_call x1, Pallas kernels: 66.9 us -> 64.7 us  [on_device(): pl.pallas_call(kernel, out_shape=jax.ShapeDtypeStruct((cams, patches, loc...]
    unnamed x1, local copies, waits for them, and re-layouts: 1.62 us -> 0.68 us
where the time goes in v4:
time: 66.2 us; the launch traced here: 66.1 us
  Pallas kernels  64.7 us (98%)
  local copies, waits for them, and re-layouts  0.68 us (1%)
    pallas_call x1, Pallas kernels, on_device(): pl.pallas_call(kernel, out_shape=jax.ShapeDtypeStruct((cams, patches, loc...  64.7 us

profile of v4, /device:TPU:193, one launch (start us, length us, event | category | flops | bytes accessed | tf_op | source)
XLA Modules:
  0.0 66.1 jit_solution(4155679455759757694)
XLA Ops:
  0.7 64.7 %shard_map.73 = bf16[6,128,128]{2,1,0:T(8,128)(2,1)S(1)} custom-call(bf16[6,128,128]{2,1,0:T(8,128)(2,1)} %bitcast.12, f32[8,2,1,128]{3,2,1,0:T(1,128)} %bitcast.13, bf16[3,8,2,128,128]{4,3,2,1,0:T(8,128)(2,1)} %bitcast.11, bf16[128,2048]{1,0:T(8,128)(2,1)} %e_hbm.1, f32[1,1]{1,0:T(1,128)} %bitcast.9.sharp_hbm, s32[2,6]{1,0:T(2,128)} %bitcast.15, ...), custom_call_target="tpu_custom_call" | custom-call | tf_op jit(solution)/shard_map/pallas_call | solution.py:403
  65.4 0.7 %copy.10 = bf16[1,6,128,128]{3,2,1,0:T(8,128)(2,1)} copy(bf16[1,6,128,128]{3,2,1,0:T(8,128)(2,1)S(1)} %bitcast.10) | data formatting | bytes 393216

commit v5 on v4

--- a/solution.py
+++ b/solution.py
@@ -22,11 +22,11 @@
 DOWN = ((4, 3), (4, 4), (3, 3))
 TREE_X = (2,)
 ORDER = (
-    "H00", "P00", "X20", "H01", "P01", "X21", "H10", "U001", "D001", "P10", "H11", "U011",
+    "H00", "P00", "H01", "P01", "X20", "H10", "X21", "U001", "D001", "P10", "H11", "U011",
     "D011", "P11", "H20", "U101", "U002", "D002", "D101", "U012", "P20", "H21",
-    "D012", "U003", "D111", "D003", "P21", "E", "D102", "U013", "D013", "C0",
-    "U111", "C2", "U201", "C1", "D112", "D201", "D004", "U102", "U014", "F0",
-    "U211", "U112", "D103", "D113", "D211", "U202", "U103", "D104", "U212", "D202",
+    "D012", "U003", "D111", "D003", "P21", "E", "D102", "U013", "D013",
+    "U111", "U201", "D112", "D201", "D004", "C0", "U102", "U014", "F0",
+    "C1", "U211", "C2", "U112", "D103", "D113", "D211", "U202", "U103", "D104", "U212", "D202",
     "U113", "D114", "F1", "U203", "D212", "U213", "D203", "U204", "D213", "U214",
     "F2",
 )
@@ -37,9 +37,9 @@
 
 
 def kernel(
-    x_hbm, gain_hbm, w_hbm, e_hbm, sharp_hbm, adj_hbm, allowed_hbm, out_hbm,
+    x_hbm, gain_hbm, w_hbm, e_hbm, sharp_hbm, adj_hbm, allowed_hbm, out_ref,
     xg, mg, mstage, kv, kc, gain_ref, w_both, e_both, scaled, x_part, x_land, m_part, m_land, m_own,
-    raw_ref, qt, top_ref, total_ref, acc_ref, out_ref, sharp_ref, adj_ref, allowed_ref,
+    raw_ref, qt, top_ref, total_ref, acc_ref, sharp_ref, adj_ref, allowed_ref,
     x_recv, x_row, x_part_recv, m_recv, m_part_recv, up_recv, dn_recv, sems,
 ):
     (x_send, x_part_send, m_send, m_part_send, up_send, dn_send, c_recv, c_send,
@@ -112,7 +112,9 @@
         acc_ref[c] = jnp.zeros((DEPTH, ROWS), jnp.float32)
     pl.semaphore_wait(barrier, HEADS + 2)
 
-    chips = [(a_, y_) for y_ in rows for a_ in (1 - a, a)]
+    near = [(a_, y_) for y_ in rows for a_ in (1 - a, a)]
+    self_chip = near[1]
+    chips = near[6:8] + near[2:6] + near[0:2]
 
     def row_push(buf, slot, send, recv):
         for y_ in rows[1:]:
@@ -126,11 +128,13 @@
             remote(x_hbm.at[mine + c], xg.at[x_slot(c, 1, a, y)], x_send, x_row.at[c, 1],
                    heads=head(1 - a, y, p)).start()
             return
-        for a_, y_ in chips:
+        for chip in chips:
+            a_, y_ = chip
             remote(x_hbm.at[theirs + c], xg.at[x_slot(c, 0, a, y)], x_send, x_recv.at[c, 0],
                    heads=head(a_, y_, p), camtime=t_x).start()
-        for n, (a_, y_) in enumerate(chips):
-            if n != 1:
+        for chip in chips:
+            a_, y_ = chip
+            if chip is not self_chip:
                 remote(x_hbm.at[mine + c], xg.at[x_slot(c, 1, a, y)], x_send, x_recv.at[c, 1],
                        heads=head(a_, y_, p)).start()
 
@@ -145,11 +149,12 @@
         )
 
     def e_push():
-        for n, (a_, y_) in enumerate(chips):
+        for chip in chips:
+            a_, y_ = chip
             for side, p_ in enumerate((p, 1 - p)):
                 src = e_hbm.at[:, pl.ds(pl.multiple_of(head(a_, y_, p_) * DEPTH, DEPTH), DEPTH)]
                 dst = e_both.at[a * ROW + y, :, side * DEPTH:(side + 1) * DEPTH]
-                if n == 1:
+                if chip is self_chip:
                     pltpu.make_async_copy(src, dst, e_recv).start()
                 else:
                     remote(src, dst, e_send, e_recv, heads=head(a_, y_, p)).start()
@@ -297,33 +302,31 @@
         cam = mine + c
         slot = m_slot(cam, a, y)
         mg[slot] = mstage[c, 1]
-        for a_, y_ in chips:
-            remote(mstage.at[c, 0], mg.at[slot], m_send, m_recv.at[c], heads=head(a_, y_, p), camtime=t_x).start()
-        for n, (a_, y_) in enumerate(chips):
-            if n != 1:
-                remote(mstage.at[c, 1], mg.at[slot], m_send, m_recv.at[c], heads=head(a_, y_, p)).start()
-
-    def m_copy(c):
-        return remote(m_part.at[c], m_land.at[c], m_part_send, m_part_recv.at[c], heads=h_sib)
-
-    def project_out_half(c):
-        arrived(xg.at[pl.ds(0, HEADS - 1)], m_recv.at[c])
-        summed = jnp.zeros((ROWS, 2 * DEPTH), jnp.float32)
+        for chip in chips:
+            a_, y_ = chip
+            remote(mstage.at[c, 0], mg.at[slot], m_send, m_recv.at[c, 0], heads=head(a_, y_, p), camtime=t_x).start()
+        for chip in chips:
+            a_, y_ = chip
+            if chip is not self_chip:
+                remote(mstage.at[c, 1], mg.at[slot], m_send, m_recv.at[c, 1], heads=head(a_, y_, p)).start()
+
+    def m_copy(c, own):
+        return remote(m_part.at[c, own], m_land.at[c, own], m_part_send, m_part_recv.at[c, own], heads=h_sib)
+
+    def project_out_half(c, own):
+        arrived(xg.at[pl.ds(0, HEADS // 2 - own)], m_recv.at[c, own])
+        cam = mine + c if own else theirs + c
+        summed = jnp.zeros((PATCH, 2 * DEPTH), jnp.float32)
         for n in range(HEADS // 2):
-            mixed = jnp.concatenate([mg[m_slot(cam, n // ROW, n % ROW)] for cam in (mine + c, theirs + c)], axis=0)
-            part = jnp.dot(mixed, e_both[n], preferred_element_type=jnp.float32)
+            part = jnp.dot(mg[m_slot(cam, n // ROW, n % ROW)], e_both[n], preferred_element_type=jnp.float32)
             summed = summed + part.astype(jnp.bfloat16).astype(jnp.float32)
-        m_part[c] = summed[:, DEPTH:]
-        m_copy(c).start()
-        m_own[c] = summed[:, :DEPTH]
-
-    def project_out(c):
-        arrived(m_land.at[c], m_part_recv.at[c])
-        summed = (m_own[c] + m_land[c]).astype(jnp.bfloat16)
-        out_ref[mine + c] = summed[:PATCH]
-        out_ref[theirs + c] = summed[PATCH:]
-        for cam in (mine + c, theirs + c):
-            pltpu.make_async_copy(out_ref.at[cam], out_hbm.at[cam], out_sem).start()
+        m_part[c, own] = summed[:, DEPTH:]
+        m_copy(c, own).start()
+        m_own[c, own] = summed[:, :DEPTH]
+
+    def project_out(c, own):
+        arrived(m_land.at[c, own], m_part_recv.at[c, own])
+        out_ref[mine + c if own else theirs + c] = (m_own[c, own] + m_land[c, own]).astype(jnp.bfloat16)
 
     x_push(0)
     for i in range(3):
@@ -358,14 +361,17 @@
         else:
             e_push()
     arrived(e_both, e_recv)
-    project_out_half(0)
-    project_out_half(1)
-    project_out(0)
-    project_out(1)
-    project_out_half(2)
-    project_out(2)
-
-    arrived(out_ref, out_sem)
+    for c in range(2):
+        for own in range(2):
+            project_out_half(c, own)
+    for c in range(2):
+        for own in range(2):
+            project_out(c, own)
+    project_out_half(2, 0)
+    project_out_half(2, 1)
+    project_out(2, 0)
+    project_out(2, 1)
+
     pieces = HEADS - 1
     arrived(xg.at[pl.ds(0, GROUP * pieces)], x_send)
     arrived(xg.at[pl.ds(0, GROUP * pieces)], m_send)
@@ -417,23 +423,22 @@
             pltpu.VMEM((ROWS, WIDTH // 2), bf16),
             pltpu.VMEM((GROUP, 2, PATCH, PART), f32),
             pltpu.VMEM((GROUP, 2, PATCH, PART), f32),
-            pltpu.VMEM((GROUP, ROWS, DEPTH), f32),
-            pltpu.VMEM((GROUP, ROWS, DEPTH), f32),
-            pltpu.VMEM((GROUP, ROWS, DEPTH), f32),
+            pltpu.VMEM((GROUP, 2, PATCH, DEPTH), f32),
+            pltpu.VMEM((GROUP, 2, PATCH, DEPTH), f32),
+            pltpu.VMEM((GROUP, 2, PATCH, DEPTH), f32),
             pltpu.VMEM((GROUP, 2, PATCH, 3 * DEPTH), f32),
             pltpu.VMEM((GROUP, DEPTH, ROWS), bf16),
             pltpu.VMEM((GROUP, 1, ROWS), f32),
             pltpu.VMEM((GROUP, 1, ROWS), f32),
             pltpu.VMEM((GROUP, DEPTH, ROWS), f32),
-            pltpu.VMEM((cams, patches, local_width), bf16),
             pltpu.SMEM((1, 1), f32),
             pltpu.SMEM((2, cams), jnp.int32),
             pltpu.SMEM((cams, PLANES * 2), jnp.int32),
             dma((GROUP, 2)),
             dma((GROUP, 2)),
             dma((GROUP, 2)),
-            dma((GROUP,)),
-            dma((GROUP,)),
+            dma((GROUP, 2)),
+            dma((GROUP, 2)),
             dma((GROUP, 2, 4)),
             dma((GROUP, 2, 4)),
             dma((SINGLE_SEMS,)),

time: 66.2 us -> 63.9 us (0.965)
  the two profiles are of different devices: /device:TPU:193 before, /device:TPU:1 now
where the time goes in v5:
time: 63.9 us; the launch traced here: 63.8 us
  Pallas kernels  62.5 us (98%)
  local copies, waits for them, and re-layouts  0.68 us (1%)
  between operations  0.66 us (1%)
    pallas_call x1, Pallas kernels, on_device(): pl.pallas_call(kernel, out_shape=jax.ShapeDtypeStruct((cams, patches, loc...  62.5 us

profile of v5, /device:TPU:1, one launch (start us, length us, event | category | flops | bytes accessed | tf_op | source)
XLA Modules:
  0.0 63.8 jit_solution(7616687396933454104)
XLA Ops:
  0.7 62.5 %shard_map.73 = bf16[6,128,128]{2,1,0:T(8,128)(2,1)S(1)} custom-call(bf16[6,128,128]{2,1,0:T(8,128)(2,1)} %bitcast.12, f32[8,2,1,128]{3,2,1,0:T(1,128)} %bitcast.13, bf16[3,8,2,128,128]{4,3,2,1,0:T(8,128)(2,1)} %bitcast.11, bf16[128,2048]{1,0:T(8,128)(2,1)} %e_hbm.1, f32[1,1]{1,0:T(1,128)} %bitcast.9.sharp_hbm, s32[2,6]{1,0:T(2,128)} %bitcast.15, ...), custom_call_target="tpu_custom_call" | custom-call | tf_op jit(solution)/shard_map/pallas_call | solution.py:409
  63.1 0.7 %copy.10 = bf16[1,6,128,128]{3,2,1,0:T(8,128)(2,1)} copy(bf16[1,6,128,128]{3,2,1,0:T(8,128)(2,1)S(1)} %bitcast.10) | data formatting | bytes 393216

commit v6 on v5

--- a/solution.py
+++ b/solution.py
@@ -39,11 +39,11 @@
 def kernel(
     x_hbm, gain_hbm, w_hbm, e_hbm, sharp_hbm, adj_hbm, allowed_hbm, out_ref,
     xg, mg, mstage, kv, kc, gain_ref, w_both, e_both, scaled, x_part, x_land, m_part, m_land, m_own,
-    raw_ref, qt, top_ref, total_ref, acc_ref, sharp_ref, adj_ref, allowed_ref,
+    raw_ref, qt, top_ref, total_ref, acc_ref, x_ref, sharp_ref, adj_ref, allowed_ref,
     x_recv, x_row, x_part_recv, m_recv, m_part_recv, up_recv, dn_recv, sems,
 ):
     (x_send, x_part_send, m_send, m_part_send, up_send, dn_send, c_recv, c_send,
-     e_recv, e_send, w_load, w_recv, w_send, gain_sem, sharp_sem, adj_sem, allowed_sem, out_sem) = [sems.at[n] for n in range(SINGLE_SEMS)]
+     e_recv, e_send, w_load, w_recv, w_send, gain_sem, sharp_sem, adj_sem, allowed_sem, x_sem) = [sems.at[n] for n in range(SINGLE_SEMS)]
     t = lax.axis_index("camtime")
     h = lax.axis_index("heads")
     z, j = t // 2, t % 2
@@ -93,6 +93,8 @@
     def m_slot(cam, a_, y_):
         return (cam * ROW + y_) * 2 + a_
 
+    x_load = pltpu.make_async_copy(x_hbm, x_ref, x_sem)
+    x_load.start()
     for c in range(GROUP):
         pltpu.make_async_copy(x_hbm.at[mine + c], xg.at[x_slot(c, 1, a, y)], (x_row if c in TREE_X else x_recv).at[c, 1]).start()
     gain_load = pltpu.make_async_copy(gain_hbm.at[:, p], gain_ref, gain_sem)
@@ -111,31 +113,32 @@
         total_ref[c] = jnp.zeros((1, ROWS), jnp.float32)
         acc_ref[c] = jnp.zeros((DEPTH, ROWS), jnp.float32)
     pl.semaphore_wait(barrier, HEADS + 2)
+    x_load.wait()
 
     near = [(a_, y_) for y_ in rows for a_ in (1 - a, a)]
     self_chip = near[1]
     chips = near[6:8] + near[2:6] + near[0:2]
 
     def row_push(buf, slot, send, recv):
-        for y_ in rows[1:]:
+        for y_ in rows[:0:-1]:
             remote(buf.at[pl.ds(slot, 2)], buf.at[pl.ds(slot, 2)], send, recv, heads=head(a, y_, p)).start()
 
     def x_push(c):
         if c in TREE_X:
             for a_ in (1 - a, a):
-                remote(x_hbm.at[theirs + c], xg.at[x_slot(c, 0, a, y)], x_send, x_row.at[c, 0],
+                remote(x_ref.at[theirs + c], xg.at[x_slot(c, 0, a, y)], x_send, x_row.at[c, 0],
                        heads=head(a_, y, p), camtime=t_x).start()
-            remote(x_hbm.at[mine + c], xg.at[x_slot(c, 1, a, y)], x_send, x_row.at[c, 1],
+            remote(x_ref.at[mine + c], xg.at[x_slot(c, 1, a, y)], x_send, x_row.at[c, 1],
                    heads=head(1 - a, y, p)).start()
             return
         for chip in chips:
             a_, y_ = chip
-            remote(x_hbm.at[theirs + c], xg.at[x_slot(c, 0, a, y)], x_send, x_recv.at[c, 0],
+            remote(x_ref.at[theirs + c], xg.at[x_slot(c, 0, a, y)], x_send, x_recv.at[c, 0],
                    heads=head(a_, y_, p), camtime=t_x).start()
         for chip in chips:
             a_, y_ = chip
             if chip is not self_chip:
-                remote(x_hbm.at[mine + c], xg.at[x_slot(c, 1, a, y)], x_send, x_recv.at[c, 1],
+                remote(x_ref.at[mine + c], xg.at[x_slot(c, 1, a, y)], x_send, x_recv.at[c, 1],
                        heads=head(a_, y_, p)).start()
 
     def x_relay(c, pos):
@@ -303,12 +306,10 @@
         slot = m_slot(cam, a, y)
         mg[slot] = mstage[c, 1]
         for chip in chips:
-            a_, y_ = chip
-            remote(mstage.at[c, 0], mg.at[slot], m_send, m_recv.at[c, 0], heads=head(a_, y_, p), camtime=t_x).start()
-        for chip in chips:
-            a_, y_ = chip
+            to = head(chip[0], chip[1], p)
+            remote(mstage.at[c, 0], mg.at[slot], m_send, m_recv.at[c, 0], heads=to, camtime=t_x).start()
             if chip is not self_chip:
-                remote(mstage.at[c, 1], mg.at[slot], m_send, m_recv.at[c, 1], heads=head(a_, y_, p)).start()
+                remote(mstage.at[c, 1], mg.at[slot], m_send, m_recv.at[c, 1], heads=to).start()
 
     def m_copy(c, own):
         return remote(m_part.at[c, own], m_land.at[c, own], m_part_send, m_part_recv.at[c, own], heads=h_sib)
@@ -431,6 +432,7 @@
             pltpu.VMEM((GROUP, 1, ROWS), f32),
             pltpu.VMEM((GROUP, 1, ROWS), f32),
             pltpu.VMEM((GROUP, DEPTH, ROWS), f32),
+            pltpu.VMEM((cams, patches, local_width), bf16),
             pltpu.SMEM((1, 1), f32),
             pltpu.SMEM((2, cams), jnp.int32),
             pltpu.SMEM((cams, PLANES * 2), jnp.int32),

time: 63.9 us -> 63.7 us (level)
  no operation moved by 1% of the time
where the time goes in v6:
time: 63.7 us
  Pallas kernels  62.3 us (98%)
  local copies, waits for them, and re-layouts  0.68 us (1%)
  between operations  0.66 us (1%)
    pallas_call x1, Pallas kernels, on_device(): pl.pallas_call(kernel, out_shape=jax.ShapeDtypeStruct((cams, patches, loc...  62.3 us

profile of v6, /device:TPU:1, one launch (start us, length us, event | category | flops | bytes accessed | tf_op | source)
XLA Modules:
  0.0 63.7 jit_solution(262831971595922522)
XLA Ops:
  0.7 62.3 %shard_map.73 = bf16[6,128,128]{2,1,0:T(8,128)(2,1)S(1)} custom-call(bf16[6,128,128]{2,1,0:T(8,128)(2,1)} %bitcast.12, f32[8,2,1,128]{3,2,1,0:T(1,128)} %bitcast.13, bf16[3,8,2,128,128]{4,3,2,1,0:T(8,128)(2,1)} %bitcast.11, bf16[128,2048]{1,0:T(8,128)(2,1)} %e_hbm.1, f32[1,1]{1,0:T(1,128)} %bitcast.9.sharp_hbm, s32[2,6]{1,0:T(2,128)} %bitcast.15, ...), custom_call_target="tpu_custom_call" | custom-call | tf_op jit(solution)/shard_map/pallas_call | solution.py:410
  63.0 0.7 %copy.10 = bf16[1,6,128,128]{3,2,1,0:T(8,128)(2,1)} copy(bf16[1,6,128,128]{3,2,1,0:T(8,128)(2,1)S(1)} %bitcast.10) | data formatting | bytes 393216
